TPU v7x, 256 devices: a whole 4x4x8 slice. The times are simulated.
256 devices in a mesh: ctx: 64 (over z, x, core), head: 4 (over y).
Axes of the slice: x: 4, y: 4, z: 8, core: 2. Of those that a mesh axis runs over, the one named last changes fastest.
Arguments:
- out_grad: bfloat16 [32768, 2560], P('ctx', 'head'), may hold values from -0.3125 to 0.3125
- out_proj: bfloat16 [2048, 2560], P('head'), may hold values from -0.125 to 0.125
- query_rows: bfloat16 [32768, 2048], P('ctx', 'head'), may hold values from -6 to 6
- key_rows: bfloat16 [32768, 2048], P('ctx', 'head'), may hold values from -6 to 6
- value_rows: bfloat16 [32768, 2048], P('ctx', 'head'), may hold values from -6 to 6
- log_decay: float32 [8, 32768], P('head', 'ctx'), as said below
- doc_starts: int32 [3], replicated, may hold values from 1 to 32767, as said below
Outputs:
- query_grad: float32 [32768, 2048], P('ctx', 'head')
- key_grad: float32 [32768, 2048], P('ctx', 'head')
- value_grad: float32 [32768, 2048], P('ctx', 'head')
Inputs may be any that keep to these rules, and one draw needn't show every extreme that they name: `doc_starts`: 3 strictly increasing token positions, each at least 1 and below 32768. `log_decay`: every entry is negative; each head's decays vary from token to token.
All inputs are finite; a program needn't handle non-finite values.
Results may differ from a plain program's by a relative error of at most 0.0049.
Values may be sent and summed in bfloat16 or wider, within the bound.
A program may use at most 192 MiB of HBM per device.

v0:
```python
import jax
import jax.numpy as jnp
from jax import lax
from jax.sharding import PartitionSpec as P

HEAD_SIZE = 256


def entering(x, axis, combine, identity, reverse):
    size, mine = (lax.axis_size(axis), lax.axis_index(axis))
    everything = jax.tree.map(lambda part: lax.all_gather(part, axis), x)
    start = jax.tree.map(
        lambda part, zero: jnp.broadcast_to(jnp.asarray(zero, part.dtype), part.shape), x, identity
    )

    def turn(k, before):
        at = size - 1 - k if reverse else k
        reached = at > mine if reverse else at < mine
        new = combine(before, jax.tree.map(lambda part: part[at], everything))
        return jax.tree.map(lambda a, b: jnp.where(reached, a, b), new, before)

    return lax.fori_loop(0, size, turn, start)


def geometry(log_block, doc_starts, offset):
    length = log_block.shape[1]
    places = offset + jnp.arange(length, dtype=jnp.int32)
    segment = jnp.sum((doc_starts[None, :] <= places[:, None]).astype(jnp.int32), axis=1)
    before = jnp.sum((doc_starts <= offset - 1).astype(jnp.int32))
    cumulative = jnp.cumsum(log_block, axis=1)
    inflow = jnp.exp(cumulative) * (segment == before).astype(jnp.float32)[None, :]
    outflow = (
        jnp.exp(cumulative[:, -1:] - cumulative)
        * (segment == segment[-1]).astype(jnp.float32)[None, :]
    )
    return (cumulative, segment, inflow, outflow)


def pair_weights(cumulative, segment):
    length = segment.shape[0]
    order = jnp.arange(length, dtype=jnp.int32)
    causal = (segment[:, None] == segment[None, :]) & (order[None, :] <= order[:, None])
    spread = cumulative[:, :, None] - cumulative[:, None, :]
    return jnp.exp(jnp.where(causal[None], spread, -1e30))


def combine(earlier, later):
    return (earlier[0] * later[0], later[0][:, None, None] * earlier[1] + later[1])


def on_device(out_grad, out_proj, query_rows, key_rows, value_rows, log_decay, doc_starts):
    length = query_rows.shape[0]
    heads_here = log_decay.shape[0]
    factor = HEAD_SIZE ** (-0.5)
    grad_sum = lax.dot_general(
        lax.all_gather(out_grad, "head", axis=1, tiled=True),
        out_proj,
        (((1,), (1,)), ((), ())),
        preferred_element_type=jnp.float32,
    )
    shaped = (length, heads_here, HEAD_SIZE)
    grad_heads = grad_sum.astype(jnp.bfloat16).reshape(shaped)
    scaled = (query_rows * factor).reshape(shaped)
    key_here = key_rows.reshape(shaped)
    value_here = value_rows.reshape(shaped)
    offset = lax.axis_index("ctx") * length
    cumulative, segment, inflow, outflow = geometry(log_decay, doc_starts, offset)
    through = inflow[:, -1]
    decayed_keys = (key_here * outflow.T[:, :, None]).astype(jnp.bfloat16)
    decayed_queries = (scaled * inflow.T[:, :, None]).astype(jnp.bfloat16)
    forward_state = jnp.einsum(
        "thd,the->hde", decayed_keys, value_here, preferred_element_type=jnp.float32
    )
    adjoint_state = jnp.einsum(
        "thd,the->hde", decayed_queries, grad_heads, preferred_element_type=jnp.float32
    )
    identity = (
        jnp.ones((heads_here,), jnp.float32),
        jnp.zeros((heads_here, HEAD_SIZE, HEAD_SIZE), jnp.float32),
    )
    state_in = entering((through, forward_state), "ctx", combine, identity, False)[1].astype(
        jnp.bfloat16
    )
    adjoint_in = entering((through, adjoint_state), "ctx", combine, identity, True)[1].astype(
        jnp.bfloat16
    )
    weights = pair_weights(cumulative, segment)
    first_mixed = (
        jnp.einsum("thd,shd->hts", grad_heads, value_here, preferred_element_type=jnp.float32)
        * weights
    ).astype(jnp.bfloat16)
    second_mixed = (
        jnp.einsum("thd,shd->hts", scaled, key_here, preferred_element_type=jnp.float32) * weights
    ).astype(jnp.bfloat16)
    query_grad = factor * (
        jnp.einsum("hts,shd->thd", first_mixed, key_here, preferred_element_type=jnp.float32)
        + inflow.T[:, :, None]
        * jnp.einsum("the,hde->thd", grad_heads, state_in, preferred_element_type=jnp.float32)
    )
    key_grad = jnp.einsum(
        "hts,thd->shd", first_mixed, scaled, preferred_element_type=jnp.float32
    ) + outflow.T[:, :, None] * jnp.einsum(
        "she,hde->shd", value_here, adjoint_in, preferred_element_type=jnp.float32
    )
    value_grad = jnp.einsum(
        "hts,the->she", second_mixed, grad_heads, preferred_element_type=jnp.float32
    ) + outflow.T[:, :, None] * jnp.einsum(
        "shd,hde->she", key_here, adjoint_in, preferred_element_type=jnp.float32
    )
    width = heads_here * HEAD_SIZE
    return (
        query_grad.reshape(length, width),
        key_grad.reshape(length, width),
        value_grad.reshape(length, width),
    )


def solution(mesh):
    return jax.shard_map(
        on_device,
        mesh=mesh,
        in_specs=(
            P("ctx", "head"),
            P("head", None),
            P("ctx", "head"),
            P("ctx", "head"),
            P("ctx", "head"),
            P("head", "ctx"),
            P(),
        ),
        out_specs=(P("ctx", "head"), P("ctx", "head"), P("ctx", "head")),
        check_vma=False,
    )
```

profile of v0, /device:TPU:1, one launch (start us, length us, event | category | flops | bytes accessed | tf_op | source)
XLA Modules:
  0.0 437.1 jit_solution(16048052460673187863)
XLA Ops:
  9.7 1.3 copy.95
  12.3 1.3 fusion.29
  13.8 1.3 compare_convert_fusion
  15.2 2.2 fusion.16
  17.4 1.9 broadcast_multiply_fusion
  19.3 1.3 copy.98
  20.6 30.9 %all-gather.7.cloned.1.call-done = bf16[512,2560]{1,0:T(8,128)(2,1)} async-done(((bf16[512,640]{1,0:T(8,128)(2,1)}), bf16[512,2560]{1,0:T(8,128)(2,1)}) %all-gather.7.cloned.1.call-update) | async-done | bytes 2621456 | tf_op jit(solution)/shard_map/all_gather | solution.py:56
  51.5 3.3 convolution_convert_fusion
  58.4 126.8 %all-reduce = f32[128]{0:T(128)S(1)} all-reduce(f32[128]{0:T(128)S(1)} %dynamic-update-slice), channel_id=2, replica_groups=mesh['ctx'=64,'head'=4] {'ctx'}, use_global_device_ids=true, to_apply=%add | all-reduce | flops 128 | bytes 1024
  185.6 2.0 multiply_convert_fusion.1
  187.6 1.5 convolution_bitcast_fusion.4
  189.5 9.0 %all-gather.9.cloned.1.call-done = f32[128,256,256]{2,1,0:T(8,128)} async-done(((f32[2,256,256]{2,1,0:T(8,128)}), f32[128,256,256]{2,1,0:T(8,128)}) %all-gather.9.cloned.1.call-update) | async-done | bytes 33554448 | tf_op jit(solution)/shard_map/all_gather | solution.py:11
  198.5 78.5 %while.30 = (s32[]{:T(128)}, f32[2,256,256]{2,1,0:T(8,128)S(1)}, s32[]{:T(128)}, f32[64,2]{1,0:T(8,128)S(1)}, f32[64,2,256,256]{3,2,1,0:T(8,128)}, /*index=5*/s32[]{:T(128)}, s32[]{:T(128)}) while((s32[]{:T(128)}, f32[2,256,256]{2,1,0:T(8,128)S(1)}, s32[]{:T(128)}, f32[64,2]{1,0:T(8,128)S(1)}, f32[64,2,256,256]{3,2,1,0:T(8,128)}, ...), condition=%wide.region_5.6_spmd.clone, body=%wide.region_4.5_spmd.clone.sunk | while | flops 524292 | bytes 1573001 | solution.py:22
  209.5 1.2 fusion.46
  210.7 1.2 fusion.46
  218.0 1.2 fusion.46
  222.9 1.2 fusion.46
  224.2 1.2 fusion.46
  227.8 1.2 fusion.46
  229.1 1.2 fusion.46
  231.5 1.2 fusion.46
  232.7 1.2 fusion.46
  233.9 1.2 fusion.46
  235.2 1.2 fusion.46
  251.0 1.3 fusion.46
  252.3 1.3 fusion.46
  253.7 1.2 fusion.46
  258.6 1.2 fusion.46
  261.0 1.2 fusion.46
  262.3 1.2 fusion.46
  267.2 1.2 fusion.46
  268.4 1.2 fusion.46
  272.1 1.3 fusion.46
  273.4 1.2 fusion.46
  277.0 2.7 fusion.10
  279.8 2.6 copy.105
  282.3 58.5 %all-gather.11.cloned.1.call-done = f32[128,256,256]{2,1,0:T(8,128)} async-done(((f32[2,256,256]{2,1,0:T(8,128)}), f32[128,256,256]{2,1,0:T(8,128)}) %all-gather.11.cloned.1.call-update) | async-done | bytes 33554448 | tf_op jit(solution)/shard_map/all_gather | solution.py:11
  340.8 78.3 %while.31 = (s32[]{:T(128)}, f32[2,256,256]{2,1,0:T(8,128)S(1)}, s32[]{:T(128)}, f32[64,2]{1,0:T(8,128)S(1)}, f32[64,2,256,256]{3,2,1,0:T(8,128)}, /*index=5*/s32[]{:T(128)}, s32[]{:T(128)}, s32[]{:T(128)}, s32[]{:T(128)}) while((s32[]{:T(128)}, f32[2,256,256]{2,1,0:T(8,128)S(1)}, s32[]{:T(128)}, f32[64,2]{1,0:T(8,128)S(1)}, ...), condition=%wide.region_7.8_spmd.clone, body=%wide.region_6.7_spmd.clone.sunk | while | flops 524296 | bytes 1573063 | solution.py:22
  342.1 1.2 fusion.47
  343.3 1.2 fusion.47
  344.5 1.2 fusion.47
  345.7 1.2 fusion.47
  347.0 1.2 fusion.47
  419.2 1.3 fusion.5
  420.5 1.3 fusion.7
  421.8 2.5 copy.106
  424.3 3.7 fusion.4
  428.1 2.5 copy.107
  (273 shorter events, 128.7 us)
Async XLA Ops:
  7.2 44.3 %copy-start = (bf16[512,2560]{1,0:T(8,128)(2,1)S(1)}, bf16[512,2560]{1,0:T(8,128)(2,1)}, u32[]{:S(2)}) copy-start(bf16[512,2560]{1,0:T(8,128)(2,1)} %param.12) | copy-start | bytes 7864324
  7.2 44.3 %all-gather.7.cloned.1.call-start = ((), (), s32[]{:S(2)}) async-start(), calls=%async_computation | async-start | bytes 3276800 | tf_op jit(solution)/shard_map/all_gather | solution.py:56
  7.9 190.6 %all-gather.9.cloned.1.call-start = ((), (), s32[]{:S(2)}) async-start(), calls=%async_computation.1 | async-start | bytes 34078720 | tf_op jit(solution)/shard_map/all_gather | solution.py:11
  11.0 6.5 %copy-start.2 = (bf16[512,512]{0,1:T(8,128)(2,1)}, bf16[512,512]{0,1:T(8,128)(2,1)S(1)}, u32[]{:S(2)}) copy-start(bf16[512,512]{0,1:T(8,128)(2,1)S(1)} %copy.95) | copy-start | bytes 1572868
  17.4 323.4 %all-gather.11.cloned.1.call-start = ((), (), s32[]{:S(2)}) async-start(), calls=%async_computation.2 | async-start | bytes 34078720 | tf_op jit(solution)/shard_map/all_gather | solution.py:11
  54.7 0.8 copy-start.4
  54.8 2.0 copy-start.7
  54.8 130.8 %copy-start.5 = (bf16[512,512]{1,0:T(8,128)(2,1)S(1)}, bf16[512,512]{1,0:T(8,128)(2,1)}, u32[]{:S(2)}) copy-start(bf16[512,512]{1,0:T(8,128)(2,1)} %param.15) | copy-start | bytes 1572868
  185.6 2.0 copy-start.3
  419.1 1.4 copy-start.6
  424.3 6.3 %copy-start.1 = (bf16[512,2560]{1,0:T(8,128)(2,1)S(1)}, bf16[512,2560]{1,0:T(8,128)(2,1)}, u32[]{:S(2)}) copy-start(bf16[512,2560]{1,0:T(8,128)(2,1)} %param.12) | copy-start | bytes 7864324
Sparse Core Ops, SparseCore 0:
  9.8 41.5 all-gather.6
  54.8 143.7 all-gather.8
  201.3 139.4 all-gather.10
where the time goes:
time: 444 us; the launch traced here: 437 us
  other arithmetic  157 us (35%)
  blocking collectives  127 us (29%)
  waiting for transfers between devices  99.1 us (22%)
  matrix products  19.5 us (4%)
  local copies, waits for them, and re-layouts  15 us (3%)
  between operations  14.6 us (3%)
  loops' own time  4.79 us (1%)
    select_n x128, other arithmetic, turn(): return jax.tree.map(lambda a, b: jnp.where(reached, a, b), new, before)  151 us
    unnamed x1, blocking collectives  127 us
    all_gather x2, waiting for transfers between devices, entering(): everything = jax.tree.map(lambda part: lax.all_gather(part, axis), x)  67.6 us
    all_gather x1, waiting for transfers between devices, on_device(): lax.all_gather(out_grad, 'head', axis=1, tiled=True)  30.9 us
    unnamed x24, local copies, waits for them, and re-layouts  10.5 us
  transfers between devices with their start and end apart: 3, of which 3 were waited for; matrix products, arithmetic and copies ran while one was open for 24% of the time, Pallas kernels for 0%

commit v1 on v0

v1 whole, which is shorter than its diff:
```python
import functools

import jax
import jax.numpy as jnp
from jax import lax
from jax.experimental import pallas as pl
from jax.experimental.pallas import tpu as pltpu
from jax.sharding import PartitionSpec as P

PLANE = 8
CHUNKS = 4
MESH = pl.DeviceIdType.MESH
F32 = jnp.float32
BF16 = jnp.bfloat16


def nn(a, b):
    return lax.dot_general(a, b, (((1,), (0,)), ((), ())), preferred_element_type=F32)


def nt(a, b):
    return lax.dot_general(a, b, (((1,), (1,)), ((), ())), preferred_element_type=F32)


def tn(a, b):
    return lax.dot_general(a, b, (((0,), (0,)), ((), ())), preferred_element_type=F32)


def kernel(
    planes, members,
    doc, ld, og, w, q, k, v,
    qg, kg, vg,
    og_v, w_v, q_v, k_v, v_v, acc, g_v, wt, sm, fm, dq, inc, outc, qg_v, kg_v, vg_v,
    t_send, t_rec, s_send, s_rec, pre, zf_send, zf_rec, za_send, za_rec, zb_send, zb_rec,
    o_send, st_in,
    local_sem, out_sem, y_send, y_rec, t_sem, c_send, c_rec,
):
    tokens, width = q_v.shape
    feats = og_v.shape[2]
    size = width // 2
    rows = s_send.shape[2]
    sub = za_send.shape[1]
    chunk = tokens // CHUNKS
    factor = size ** -0.5
    ctx, y = lax.axis_index("ctx"), lax.axis_index("head")
    z, p = ctx // members, ctx % members
    right, left = (y + 1) % 4, (y + 3) % 4
    owners = (y, left, right, (y + 2) % 4)

    loads = [pltpu.make_async_copy(og, og_v.at[0], local_sem.at[0])]
    for i, (src, dst) in enumerate(((k, k_v), (v, v_v), (q, q_v))):
        loads.append(pltpu.make_async_copy(src, dst, local_sem.at[1 + i]))
    for i in range(4):
        start = pl.multiple_of(owners[i] * feats, 128)
        loads.append(pltpu.make_async_copy(w.at[:, pl.ds(start, feats)], w_v.at[i], local_sem.at[4 + i]))
    for load in loads:
        load.start()

    barrier = pltpu.get_barrier_semaphore()
    for other in (left, right):
        pl.semaphore_signal(barrier, inc=1, device_id=(ctx, other), device_id_type=MESH)

    def greet_plane(d, c):
        pl.semaphore_signal(barrier, inc=1, device_id=(z * members + (p + d) % members, y), device_id_type=MESH)
        return c

    def greet_z(d, c):
        pl.semaphore_signal(barrier, inc=1, device_id=(((z + d) % planes) * members + p, y), device_id_type=MESH)
        return c

    lax.fori_loop(1, members, greet_plane, 0)
    lax.fori_loop(1, planes, greet_z, 0)
    pl.semaphore_wait(barrier, 2 + (members - 1) + (planes - 1))

    def hop(src_slot, dst_slot, c, to, lane):
        at = pl.ds(c * chunk, chunk)
        return pltpu.make_async_remote_copy(
            src_ref=og_v.at[src_slot, at], dst_ref=og_v.at[dst_slot, at],
            send_sem=y_send.at[lane, c], recv_sem=y_rec.at[dst_slot - 1, c],
            device_id=(ctx, to), device_id_type=MESH,
        )

    to_right = [hop(0, 1, c, right, 0) for c in range(CHUNKS)]
    to_left = [hop(0, 2, c, left, 1) for c in range(CHUNKS)]
    onward = [hop(1, 3, c, right, 2) if c < CHUNKS // 2 else hop(2, 3, c, left, 2) for c in range(CHUNKS)]
    loads[0].wait()
    for c in range(CHUNKS):
        to_right[c].start()
        to_left[CHUNKS - 1 - c].start()

    offset = ctx * tokens
    lane = lax.broadcasted_iota(jnp.int32, (8, tokens), 1)
    docs = [doc[i] for i in range(doc.shape[0])]

    def segment(places):
        total = jnp.zeros(places.shape, jnp.int32)
        for d in docs:
            total = total + (d <= places).astype(jnp.int32)
        return total

    def segment_at(place):
        total = jnp.int32(0)
        for d in docs:
            total = total + (d <= place).astype(jnp.int32)
        return total

    before, last = segment_at(offset - 1), segment_at(offset + tokens - 1)
    seg_row = segment(offset + lane)[0:1]
    row_at = lax.broadcasted_iota(jnp.int32, (tokens, tokens), 0)
    col_at = lax.broadcasted_iota(jnp.int32, (tokens, tokens), 1)
    seg_col = segment(offset + lax.broadcasted_iota(jnp.int32, (tokens, 1), 0))
    in_row = (seg_row == before).astype(F32)
    in_col = (seg_col == before).astype(F32)
    out_col = (seg_col == last).astype(F32)
    same = (seg_col == seg_row) & (col_at <= row_at)
    cums = []
    for h in range(2):
        cum = jnp.broadcast_to(ld[h : h + 1, :], (8, tokens))
        step = 1
        while step < tokens:
            cum = cum + jnp.where(lane >= step, pltpu.roll(cum, step, 1), 0.0)
            step *= 2
        whole = jnp.sum(jnp.where(lane == tokens - 1, cum, 0.0), axis=1, keepdims=True)
        through = jnp.exp(whole) * jnp.where(before == last, 1.0, 0.0)
        t_send[h] = jnp.broadcast_to(through, (8, t_send.shape[2]))
        cum_row = cum[0:1]
        cum_col = jnp.sum(jnp.where(row_at == col_at, cum_row, 0.0), axis=1, keepdims=True)
        inc[h] = jnp.exp(cum_col) * in_col
        outc[h] = jnp.exp(whole[0:1] - cum_col) * out_col
        cums.append((cum_row, cum_col))

    def plane_copy(j, src, dst, send, recv):
        return pltpu.make_async_remote_copy(
            src_ref=src, dst_ref=dst, send_sem=send, recv_sem=recv,
            device_id=(z * members + j, y), device_id_type=MESH,
        )

    def z_copy(j, src, dst, send, recv):
        return pltpu.make_async_remote_copy(
            src_ref=src, dst_ref=dst, send_sem=send, recv_sem=recv,
            device_id=(j * members + p, y), device_id_type=MESH,
        )

    def send_plane(src, dst, send, recv, index=lambda j: j):
        def one(d, c):
            j = (p + d) % members
            plane_copy(j, src.at[index(j)], dst.at[p], send, recv).start()
            return c

        lax.fori_loop(1, members, one, 0)

    def send_z(src, dst, send, recv):
        def one(d, c):
            j = (z + d) % planes
            z_copy(j, src.at[j], dst.at[z], send, recv).start()
            return c

        lax.fori_loop(1, planes, one, 0)

    def arrived(ref, count, sem):
        part = ref.at[pl.ds(0, count)]
        pltpu.make_async_copy(part, part, sem).wait()

    heads_per = members // 2
    send_plane(t_send, t_rec, t_sem.at[0], t_sem.at[1], lambda j: j // heads_per)
    t_rec[p] = t_send[p // heads_per]

    def first(direction, h, state):
        s_send[direction, pl.ds(h * heads_per, heads_per)] = state.astype(BF16).reshape(heads_per, rows, size)

    def first_send(direction):
        send_plane(s_send.at[direction], s_rec.at[direction], c_send.at[direction, 0], c_rec.at[direction, 0])
        s_rec[direction, p] = s_send[direction, p]

    def second_send(direction):
        arrived(s_rec.at[direction], members - 1, c_rec.at[direction, 0])
        run = jnp.zeros((rows, size), F32)
        decay = jnp.ones((1, 1), F32)
        order = range(members) if direction == 0 else reversed(range(members))
        for i in order:
            pre[direction, i] = run
            t = t_rec[i, 0:1, 0:1]
            run = t * run + s_rec[direction, i].astype(F32)
            decay = decay * t
        parts = run.reshape(planes, sub, size)
        if direction == 0:
            zf_send[:, 0:sub] = parts
            zf_send[:, sub:] = jnp.broadcast_to(decay.reshape(1, 1, 1), (planes, 8, size))
            send, rec = zf_send, zf_rec
        else:
            za_send[...] = parts
            send, rec = za_send, za_rec
        send_z(send, rec, c_send.at[direction, 1], c_rec.at[direction, 1])
        rec[z] = send[z]

    def third_send(direction):
        rec = za_rec if direction else zf_rec
        arrived(rec, planes - 1, c_rec.at[direction, 1])
        run = jnp.zeros((sub, size), F32)
        order = range(planes) if direction == 0 else reversed(range(planes))
        for i in order:
            zb_send[direction, i] = run
            run = zf_rec[i, sub : sub + 1] * run + rec[i, 0:sub]
        send_z(zb_send.at[direction], zb_rec.at[direction], c_send.at[direction, 2], c_rec.at[direction, 2])
        zb_rec[direction, z] = zb_send[direction, z]

    def fourth_send(direction):
        arrived(zb_rec.at[direction], planes - 1, c_rec.at[direction, 2])
        entering = zb_rec[direction].reshape(rows, size)
        decay = jnp.ones((1, 1), F32)
        order = range(members) if direction == 0 else reversed(range(members))
        for i in order:
            o_send[direction, i] = (pre[direction, i] + decay * entering).astype(BF16)
            decay = decay * t_rec[i, 0:1, 0:1]
        send_plane(o_send.at[direction], st_in.at[direction], c_send.at[direction, 3], c_rec.at[direction, 3])
        st_in[direction, p] = o_send[direction, p]

    def state(direction, h):
        arr = st_in[direction, pl.ds(h * heads_per, heads_per)]
        return arr.reshape(size, size)

    def cols(h):
        return slice(h * size, (h + 1) * size)

    loads[1].wait()
    loads[2].wait()
    for h in range(2):
        decayed = (k_v[:, cols(h)].astype(F32) * outc[h]).astype(BF16)
        first(0, h, tn(decayed, v_v[:, cols(h)]))
    first_send(0)

    loads[3].wait()
    q_v[...] = q_v[...] * jnp.asarray(factor, BF16)
    for h in range(2):
        dq[:, cols(h)] = (q_v[:, cols(h)].astype(F32) * inc[h]).astype(BF16)
        cum_row, cum_col = cums[h]
        wt[h] = jnp.exp(jnp.where(same, cum_col - cum_row, -1e30))
        sm[h] = (nt(q_v[:, cols(h)], k_v[:, cols(h)]) * wt[h]).astype(BF16)
    loads[4].wait()
    acc[...] = nt(og_v[0], w_v[0])

    arrived(t_rec, members - 1, t_sem.at[1])
    second_send(0)

    for i in range(1, 4):
        loads[4 + i].wait()

    def add(slot, c):
        at = slice(c * chunk, (c + 1) * chunk)
        acc[at, :] += nt(og_v[slot, at], w_v[slot])

    half = CHUNKS // 2
    for c in range(half):
        to_right[c].wait_recv()
        onward[c].start()
        to_left[CHUNKS - 1 - c].wait_recv()
        onward[CHUNKS - 1 - c].start()
        add(1, c)
        add(2, CHUNKS - 1 - c)
        if c == 0:
            third_send(0)
    fourth_send(0)
    for c in range(half):
        to_right[half + c].wait_recv()
        add(1, half + c)
        to_left[half - 1 - c].wait_recv()
        add(2, half - 1 - c)

    adj = [jnp.zeros((size, size), F32), jnp.zeros((size, size), F32)]
    for c in range(half):
        for at in (c, CHUNKS - 1 - c):
            onward[at].wait_recv()
            span = slice(at * chunk, (at + 1) * chunk)
            here = (acc[span, :] + nt(og_v[3, span], w_v[3])).astype(BF16)
            g_v[span, :] = here
            for h in range(2):
                adj[h] = adj[h] + tn(dq[span, cols(h)], here[:, cols(h)])
    for h in range(2):
        first(1, h, adj[h])
    first_send(1)

    outs = []

    def put(src, dst, h, i):
        copy = pltpu.make_async_copy(src.at[:, cols(h)], dst.at[:, cols(h)], out_sem.at[i, h])
        copy.start()
        outs.append(copy)

    for h in range(2):
        fm[h] = (nt(g_v[:, cols(h)], v_v[:, cols(h)]) * wt[h]).astype(BF16)
    second_send(1)
    arrived(st_in.at[0], members - 1, c_rec.at[0, 3])
    for h in range(2):
        entering = nt(g_v[:, cols(h)], state(0, h))
        qg_v[:, cols(h)] = factor * (nn(fm[h], k_v[:, cols(h)]) + inc[h] * entering)
        put(qg_v, qg, h, 0)
    third_send(1)
    for h in range(2):
        kg_v[:, cols(h)] = tn(fm[h], q_v[:, cols(h)])
    fourth_send(1)
    for h in range(2):
        vg_v[:, cols(h)] = tn(sm[h], g_v[:, cols(h)])

    for copy in to_right + to_left + onward:
        copy.wait_send()
    arrived(t_rec, members - 1, t_sem.at[0])
    for direction in range(2):
        zs = za_send if direction else zf_send
        arrived(s_send.at[direction], members - 1, c_send.at[direction, 0])
        arrived(zs, planes - 1, c_send.at[direction, 1])
        arrived(zb_send.at[direction], planes - 1, c_send.at[direction, 2])
        arrived(o_send.at[direction], members - 1, c_send.at[direction, 3])

    arrived(st_in.at[1], members - 1, c_rec.at[1, 3])
    for h in range(2):
        kg_v[:, cols(h)] += outc[h] * nt(v_v[:, cols(h)], state(1, h))
        put(kg_v, kg, h, 1)
        vg_v[:, cols(h)] += outc[h] * nn(k_v[:, cols(h)], state(1, h))
        put(vg_v, vg, h, 2)
    for copy in outs:
        copy.wait()


def on_device(planes, members, out_grad, out_proj, query_rows, key_rows, value_rows, log_decay, doc_starts):
    tokens, width = query_rows.shape
    feats = out_grad.shape[1]
    size = width // 2
    rows = width // members
    sub = rows // planes
    any_space = pl.BlockSpec(memory_space=pl.ANY)
    result = jax.ShapeDtypeStruct((tokens, width), F32)
    lanes = 128
    scratch = [
        pltpu.VMEM((4, tokens, feats), BF16),
        pltpu.VMEM((4, width, feats), BF16),
        pltpu.VMEM((tokens, width), BF16),
        pltpu.VMEM((tokens, width), BF16),
        pltpu.VMEM((tokens, width), BF16),
        pltpu.VMEM((tokens, width), F32),
        pltpu.VMEM((tokens, width), BF16),
        pltpu.VMEM((2, tokens, tokens), F32),
        pltpu.VMEM((2, tokens, tokens), BF16),
        pltpu.VMEM((2, tokens, tokens), BF16),
        pltpu.VMEM((tokens, width), BF16),
        pltpu.VMEM((2, tokens, 1), F32),
        pltpu.VMEM((2, tokens, 1), F32),
        pltpu.VMEM((tokens, width), F32),
        pltpu.VMEM((tokens, width), F32),
        pltpu.VMEM((tokens, width), F32),
        pltpu.VMEM((2, 8, lanes), F32),
        pltpu.VMEM((members, 8, lanes), F32),
        pltpu.VMEM((2, members, rows, size), BF16),
        pltpu.VMEM((2, members, rows, size), BF16),
        pltpu.VMEM((2, members, rows, size), F32),
        pltpu.VMEM((planes, sub + 8, size), F32),
        pltpu.VMEM((planes, sub + 8, size), F32),
        pltpu.VMEM((planes, sub, size), F32),
        pltpu.VMEM((planes, sub, size), F32),
        pltpu.VMEM((2, planes, sub, size), F32),
        pltpu.VMEM((2, planes, sub, size), F32),
        pltpu.VMEM((2, members, rows, size), BF16),
        pltpu.VMEM((2, members, rows, size), BF16),
        pltpu.SemaphoreType.DMA((8,)),
        pltpu.SemaphoreType.DMA((3, 2)),
        pltpu.SemaphoreType.DMA((3, CHUNKS)),
        pltpu.SemaphoreType.DMA((3, CHUNKS)),
        pltpu.SemaphoreType.DMA((2,)),
        pltpu.SemaphoreType.DMA((2, 4)),
        pltpu.SemaphoreType.DMA((2, 4)),
    ]
    return pl.pallas_call(
        functools.partial(kernel, planes, members),
        out_shape=(result, result, result),
        in_specs=[
            pl.BlockSpec(memory_space=pltpu.SMEM),
            pl.BlockSpec(memory_space=pltpu.VMEM),
        ] + [any_space] * 5,
        out_specs=(any_space, any_space, any_space),
        scratch_shapes=scratch,
        compiler_params=pltpu.CompilerParams(
            collective_id=0, has_side_effects=True, vmem_limit_bytes=56 * 1024 * 1024
        ),
        name="retention_backward",
    )(doc_starts, log_decay, out_grad, out_proj, query_rows, key_rows, value_rows)


def solution(mesh):
    members = PLANE
    planes = mesh.shape["ctx"] // members
    return jax.shard_map(
        functools.partial(on_device, planes, members),
        mesh=mesh,
        in_specs=(
            P("ctx", "head"),
            P("head", None),
            P("ctx", "head"),
            P("ctx", "head"),
            P("ctx", "head"),
            P("head", "ctx"),
            P(),
        ),
        out_specs=(P("ctx", "head"), P("ctx", "head"), P("ctx", "head")),
        check_vma=False,
    )
```

time: 444 us -> 61.6 us (0.14); the launches traced: 437 us -> 61.5 us
  other arithmetic: 157 us -> 0 us
  blocking collectives: 127 us -> 0 us
  waiting for transfers between devices: 99.1 us -> 0 us
  Pallas kernels: 0 us -> 56.5 us
  matrix products: 19.5 us -> 0 us
  between operations: 14.6 us -> 0.66 us
  local copies, waits for them, and re-layouts: 15 us -> 4.36 us
  loops' own time: 4.79 us -> 0 us
    select_n x128 -> x0, other arithmetic: 151 us -> none  [turn(): return jax.tree.map(lambda a, b: jnp.where(reached, a, b), new, before)]
    unnamed x1 -> x0, blocking collectives: 127 us -> none
    all_gather x3 -> x0, waiting for transfers between devices: 98.4 us -> none  [the longest x2 67.6 us: entering(): everything = jax.tree.map(lambda part: lax.all_gather(part, axis), x)]
    pallas_call x0 -> x1, Pallas kernels: none -> 56.5 us  [on_device(): pl.pallas_call(functools.partial(kernel, planes, members), out_shape=(res...]
    dot_general x10 -> x0, matrix products: 19.5 us -> none  [the longest x1 3.72 us: on_device(): jnp.einsum('hts,the->she', second_mixed, grad_heads, preferred_element_ty...]
    unnamed x24 -> x7, local copies, waits for them, and re-layouts: 10.5 us -> 4.36 us
    another operation x2 -> x0, loops' own time: 4.79 us -> none  [entering(): return lax.fori_loop(0, size, turn, start)]
  transfers between devices with their start and end apart: 3 -> 0, of which waited for: 3 -> 0; matrix products, arithmetic and copies ran while one was open for 24% -> 0% of each run, Pallas kernels for 0% -> 0%
where the time goes in v1:
time: 61.6 us; the launch traced here: 61.5 us
  Pallas kernels  56.5 us (92%)
  local copies, waits for them, and re-layouts  4.36 us (7%)
  between operations  0.66 us (1%)
    pallas_call x1, Pallas kernels, on_device(): pl.pallas_call(functools.partial(kernel, planes, members), out_shape=(res...  56.5 us
    unnamed x7, local copies, waits for them, and re-layouts  4.36 us

profile of v1, /device:TPU:1, one launch (start us, length us, event | category | flops | bytes accessed | tf_op | source)
XLA Modules:
  0.0 61.5 jit_solution(10105148241445689074)
XLA Ops:
  0.6 56.5 %retention_backward.1 = (f32[512,512]{1,0:T(8,128)}, f32[512,512]{1,0:T(8,128)}, f32[512,512]{1,0:T(8,128)}) custom-call(s32[3]{0:T(128)} %doc.1, f32[2,512]{1,0:T(2,128)} %ld.1, bf16[512,640]{1,0:T(8,128)(2,1)} %og.1, bf16[512,2560]{1,0:T(8,128)(2,1)} %w.1, bf16[512,512]{1,0:T(8,128)(2,1)} %q.1, bf16[512,512]{1,0:T(8,128)(2,1)} %k.1, bf16[512,512]{1,0:T(8,128)(2,1)} %v.1), custom_call_target="tpu_custom_call" | custom-call | tf_op jit(solution)/shard_map/retention_backward/pallas_call | solution.py:371
  57.2 0.0 copy-start.1
  57.2 0.0 copy-start
  57.2 2.4 %copy.13 = f32[512,512]{1,0:T(8,128)} copy(f32[512,512]{1,0:T(8,128)} %get-tuple-element.6) | data formatting | bytes 2097152
  59.6 0.0 copy-done.1
  59.6 1.0 %copy.14 = f32[512,512]{1,0:T(8,128)} copy(f32[512,512]{1,0:T(8,128)S(1)} %copy-done.1) | data formatting | bytes 2097152
  60.6 0.0 copy-done
  60.6 1.0 %copy.15 = f32[512,512]{1,0:T(8,128)} copy(f32[512,512]{1,0:T(8,128)S(1)} %copy-done) | data formatting | bytes 2097152
Async XLA Ops:
  57.2 2.4 %copy-start.1 = (f32[512,512]{1,0:T(8,128)S(1)}, f32[512,512]{1,0:T(8,128)}, u32[]{:S(2)}) copy-start(f32[512,512]{1,0:T(8,128)} %get-tuple-element.7) | copy-start | bytes 3145732
  57.2 3.4 %copy-start = (f32[512,512]{1,0:T(8,128)S(1)}, f32[512,512]{1,0:T(8,128)}, u32[]{:S(2)}) copy-start(f32[512,512]{1,0:T(8,128)} %get-tuple-element.8) | copy-start | bytes 3145732

commit v2 on v1

v2 whole, which is shorter than its diff:
```python
import functools

import jax
import jax.numpy as jnp
from jax import lax
from jax.experimental import pallas as pl
from jax.experimental.pallas import tpu as pltpu
from jax.sharding import PartitionSpec as P

PLANE = 4
CHUNKS = 4
MESH = pl.DeviceIdType.MESH
F32 = jnp.float32
BF16 = jnp.bfloat16


def nn(a, b):
    return lax.dot_general(a, b, (((1,), (0,)), ((), ())), preferred_element_type=F32)


def nt(a, b):
    return lax.dot_general(a, b, (((1,), (1,)), ((), ())), preferred_element_type=F32)


def tn(a, b):
    return lax.dot_general(a, b, (((0,), (0,)), ((), ())), preferred_element_type=F32)


def far_first(n, size):
    half = size // 2
    return half + lax.rem(n + 1, 2) * (n // 2) - lax.rem(n, 2) * ((n + 1) // 2)


def kernel(
    planes, lines,
    doc, ld, og, w, q, k, v,
    qg, kg, vg, adjoint, outflow,
    og_v, w_v, q_v, k_v, v_v, acc, g_v, wt, sm, fm, dq, inc, outc, qg_v, kg_v, vg_v, oc_v,
    t_send, t_other, tc_send, t_rec, own, core_send, core_rec, ch_send, ch_rec, en_send, en_rec,
    back_send, st_in,
    local_sem, out_sem, y_send, y_rec, t_sem, c_send, c_rec,
):
    tokens, width = q_v.shape
    feats = og_v.shape[2]
    size = width // 2
    chips, height, wide = ch_send.shape[1:]
    chunk = tokens // CHUNKS
    factor = size ** -0.5
    ctx, y = lax.axis_index("ctx"), lax.axis_index("head")
    chip, core = ctx // 2, ctx % 2
    z, x = chip // lines, chip % lines
    first_core = core == 0
    other = chip * 2 + 1 - core
    right, left = (y + 1) % 4, (y + 3) % 4
    owners = (y, left, right, (y + 2) % 4)

    loads = [pltpu.make_async_copy(og, og_v.at[0], local_sem.at[0])]
    for i, (src, dst) in enumerate(((k, k_v), (v, v_v), (q, q_v))):
        loads.append(pltpu.make_async_copy(src, dst, local_sem.at[1 + i]))
    for i in range(4):
        start = pl.multiple_of(owners[i] * feats, 128)
        loads.append(pltpu.make_async_copy(w.at[:, pl.ds(start, feats)], w_v.at[i], local_sem.at[4 + i]))
    for load in loads:
        load.start()

    def partner(n):
        there = (z + far_first(n // lines, planes)) % planes
        return there * lines + (x + far_first(n % lines, lines)) % lines

    barrier = pltpu.get_barrier_semaphore()

    def greet(n, c):
        pl.semaphore_signal(barrier, inc=1, device_id=(partner(n) * 2 + core, y), device_id_type=MESH)
        return c

    lax.fori_loop(0, chips - 1, greet, 0)
    for near in ((ctx, left), (ctx, right), (other, y)):
        pl.semaphore_signal(barrier, inc=1, device_id=near, device_id_type=MESH)
    pl.semaphore_wait(barrier, 3 + chips - 1)

    def hop(src_slot, dst_slot, c, to, lane):
        at = pl.ds(c * chunk, chunk)
        return pltpu.make_async_remote_copy(
            src_ref=og_v.at[src_slot, at], dst_ref=og_v.at[dst_slot, at],
            send_sem=y_send.at[lane, c], recv_sem=y_rec.at[dst_slot - 1, c],
            device_id=(ctx, to), device_id_type=MESH,
        )

    to_right = [hop(0, 1, c, right, 0) for c in range(CHUNKS)]
    to_left = [hop(0, 2, c, left, 1) for c in range(CHUNKS)]
    onward = [hop(1, 3, c, right, 2) if c < CHUNKS // 2 else hop(2, 3, c, left, 2) for c in range(CHUNKS)]
    loads[0].wait()
    for c in range(CHUNKS):
        to_right[c].start()
        to_left[CHUNKS - 1 - c].start()

    offset = ctx * tokens
    lane = lax.broadcasted_iota(jnp.int32, (8, tokens), 1)
    docs = [doc[i] for i in range(doc.shape[0])]

    def segment(places):
        total = jnp.zeros(places.shape, jnp.int32)
        for d in docs:
            total = total + (d <= places).astype(jnp.int32)
        return total

    def segment_at(place):
        total = jnp.int32(0)
        for d in docs:
            total = total + (d <= place).astype(jnp.int32)
        return total

    before, last = segment_at(offset - 1), segment_at(offset + tokens - 1)
    seg_row = segment(offset + lane)[0:1]
    row_at = lax.broadcasted_iota(jnp.int32, (tokens, tokens), 0)
    col_at = lax.broadcasted_iota(jnp.int32, (tokens, tokens), 1)
    seg_col = segment(offset + lax.broadcasted_iota(jnp.int32, (tokens, 1), 0))
    in_col = (seg_col == before).astype(F32)
    out_col = (seg_col == last).astype(F32)
    same = (seg_col == seg_row) & (col_at <= row_at)
    cums = []
    for h in range(2):
        cum = jnp.broadcast_to(ld[h : h + 1, :], (8, tokens))
        step = 1
        while step < tokens:
            cum = cum + jnp.where(lane >= step, pltpu.roll(cum, step, 1), 0.0)
            step *= 2
        whole = jnp.sum(jnp.where(lane == tokens - 1, cum, 0.0), axis=1, keepdims=True)
        through = jnp.exp(whole) * jnp.where(before == last, 1.0, 0.0)
        t_send[h] = jnp.broadcast_to(through, (8, t_send.shape[2]))
        cum_row = cum[0:1]
        cum_col = jnp.sum(jnp.where(row_at == col_at, cum_row, 0.0), axis=1, keepdims=True)
        inc[h] = jnp.exp(cum_col) * in_col
        outc[h] = jnp.exp(whole[0:1] - cum_col) * out_col
        cums.append((cum_row, cum_col))

    def to_core(src, dst, send, recv):
        return pltpu.make_async_remote_copy(
            src_ref=src, dst_ref=dst, send_sem=send, recv_sem=recv,
            device_id=(other, y), device_id_type=MESH,
        )

    def to_chips(src, dst, send, recv, index):
        def one(n, c):
            j = partner(n)
            pltpu.make_async_remote_copy(
                src_ref=src.at[index(j)], dst_ref=dst.at[chip], send_sem=send, recv_sem=recv,
                device_id=(j * 2 + core, y), device_id_type=MESH,
            ).start()
            return c

        lax.fori_loop(0, chips - 1, one, 0)

    def arrived(ref, count, sem):
        part = ref.at[pl.ds(0, count)]
        pltpu.make_async_copy(part, part, sem).wait()

    t_copy = to_core(t_send.at[1 - core], t_other, t_sem.at[0], t_sem.at[1])
    t_copy.start()

    def decay(ref):
        return ref[0:1, 0:1]

    def core_copy(direction):
        return to_core(
            core_send.at[direction], core_rec.at[direction], c_send.at[direction, 0], c_rec.at[direction, 0]
        )

    def back_copy(direction):
        return to_core(
            back_send.at[direction], st_in.at[direction, core], c_send.at[direction, 3], c_rec.at[direction, 3]
        )

    def first_send(direction):
        core_send[direction] = own[direction, 1 - core].astype(BF16)
        core_copy(direction).start()

    def pieces(ref, direction, whole):
        half = chips // 2 if chips > 1 else 1
        for i in range(2):
            part = whole[:, i * wide : (i + 1) * wide]
            ref[direction, i * half : (i + 1) * half] = part.reshape(half, height, wide)

    def second_send(direction):
        core_copy(direction).wait_recv()
        mine, theirs = own[direction, core], core_rec[direction].astype(F32)
        earlier = first_core if direction == 0 else jnp.logical_not(first_core)
        a = jnp.where(earlier, decay(t_other), 1.0)
        b = jnp.where(earlier, 1.0, decay(t_send.at[core]))
        pieces(ch_send, direction, (a * mine + b * theirs).astype(BF16))
        to_chips(
            ch_send.at[direction], ch_rec.at[direction], c_send.at[direction, 1], c_rec.at[direction, 1],
            lambda j: j,
        )
        ch_rec[direction, chip] = ch_send[direction, chip]

    def third_send(direction):
        arrived(ch_rec.at[direction], chips - 1, c_rec.at[direction, 1])
        run = jnp.zeros((height // 8, 8, wide), F32)
        for i in range(chips) if direction == 0 else reversed(range(chips)):
            en_send[direction, i] = run.reshape(height, wide).astype(BF16)
            here = ch_rec[direction, i].astype(F32).reshape(height // 8, 8, wide)
            run = t_rec[i, :, 0:wide] * run + here
        to_chips(
            en_send.at[direction], en_rec.at[direction], c_send.at[direction, 2], c_rec.at[direction, 2],
            lambda j: j,
        )
        en_rec[direction, chip] = en_send[direction, chip]

    def fourth_send(direction):
        arrived(en_rec.at[direction], chips - 1, c_rec.at[direction, 2])
        half = chips // 2
        parts = [en_rec[direction, i * half : (i + 1) * half].reshape(size, wide) for i in range(2)]
        entering = jnp.concatenate(parts, axis=1).astype(F32)
        earlier = first_core if direction == 0 else jnp.logical_not(first_core)
        a = jnp.where(earlier, decay(t_send.at[core]), 1.0)
        b = jnp.where(earlier, 1.0, 0.0)
        back_send[direction] = (a * entering + b * own[direction, core]).astype(BF16)
        back_copy(direction).start()
        a = jnp.where(earlier, 1.0, decay(t_other))
        st_in[direction, core] = (a * entering + (1.0 - b) * core_rec[direction].astype(F32)).astype(BF16)

    def cols(h):
        return slice(h * size, (h + 1) * size)

    loads[1].wait()
    loads[2].wait()
    for h in range(2):
        decayed = (k_v[:, cols(h)].astype(F32) * outc[h]).astype(BF16)
        own[0, h] = tn(decayed, v_v[:, cols(h)])
    first_send(0)
    t_copy.wait_recv()
    tc_send[...] = t_send[core] * t_other[...]
    to_chips(tc_send, t_rec, t_sem.at[2], t_sem.at[3], lambda j: slice(None))
    t_rec[chip] = tc_send[...]
    second_send(0)

    loads[3].wait()
    q_v[...] = q_v[...] * jnp.asarray(factor, BF16)
    at_lane = lax.broadcasted_iota(jnp.int32, oc_v.shape, 1)
    oc_v[...] = jnp.where(at_lane == 0, outc[0], outc[1])
    for h in range(2):
        dq[:, cols(h)] = (q_v[:, cols(h)].astype(F32) * inc[h]).astype(BF16)
        cum_row, cum_col = cums[h]
        wt[h] = jnp.exp(jnp.where(same, cum_col - cum_row, -1e30))
        sm[h] = (nt(q_v[:, cols(h)], k_v[:, cols(h)]) * wt[h]).astype(BF16)
    loads[4].wait()
    acc[...] = nt(og_v[0], w_v[0])
    for i in range(1, 4):
        loads[4 + i].wait()

    def add(slot, c):
        at = slice(c * chunk, (c + 1) * chunk)
        acc[at, :] += nt(og_v[slot, at], w_v[slot])

    half = CHUNKS // 2
    for c in range(half):
        to_right[c].wait_recv()
        onward[c].start()
        to_left[CHUNKS - 1 - c].wait_recv()
        onward[CHUNKS - 1 - c].start()
        add(1, c)
        add(2, CHUNKS - 1 - c)
        if c == 0:
            arrived(t_rec, chips - 1, t_sem.at[3])
            third_send(0)
    for c in range(half):
        to_right[half + c].wait_recv()
        add(1, half + c)
        to_left[half - 1 - c].wait_recv()
        add(2, half - 1 - c)
        if c == 0:
            fourth_send(0)

    adj = [jnp.zeros((size, size), F32), jnp.zeros((size, size), F32)]
    for c in range(half):
        for at in (c, CHUNKS - 1 - c):
            onward[at].wait_recv()
            span = slice(at * chunk, (at + 1) * chunk)
            here = (acc[span, :] + nt(og_v[3, span], w_v[3])).astype(BF16)
            g_v[span, :] = here
            for h in range(2):
                adj[h] = adj[h] + tn(dq[span, cols(h)], here[:, cols(h)])
    for h in range(2):
        own[1, h] = adj[h]
    first_send(1)

    outs = [pltpu.make_async_copy(oc_v, outflow, out_sem.at[3, 0])]
    outs[0].start()

    def put(src, dst, h, i):
        copy = pltpu.make_async_copy(src.at[:, cols(h)], dst.at[:, cols(h)], out_sem.at[i, h])
        copy.start()
        outs.append(copy)

    second_send(1)
    for h in range(2):
        fm[h] = (nt(g_v[:, cols(h)], v_v[:, cols(h)]) * wt[h]).astype(BF16)
    back_copy(0).wait_recv()
    for h in range(2):
        entering = nt(g_v[:, cols(h)], st_in[0, h])
        qg_v[:, cols(h)] = factor * (nn(fm[h], k_v[:, cols(h)]) + inc[h] * entering)
        put(qg_v, qg, h, 0)
    third_send(1)
    for h in range(2):
        kg_v[:, cols(h)] = tn(fm[h], q_v[:, cols(h)])
        put(kg_v, kg, h, 1)
        vg_v[:, cols(h)] = tn(sm[h], g_v[:, cols(h)])
        put(vg_v, vg, h, 2)

    for copy in to_right + to_left + onward + [t_copy]:
        copy.wait_send()
    arrived(t_rec, chips - 1, t_sem.at[2])
    for direction in range(2):
        core_copy(direction).wait_send()
        arrived(ch_send.at[direction], chips - 1, c_send.at[direction, 1])
    arrived(en_send.at[0], chips - 1, c_send.at[0, 2])
    back_copy(0).wait_send()

    fourth_send(1)
    arrived(en_send.at[1], chips - 1, c_send.at[1, 2])
    for copy in outs:
        copy.wait()
    back_copy(1).wait()
    last_copy = pltpu.make_async_copy(st_in.at[1], adjoint, out_sem.at[3, 1])
    last_copy.start()
    last_copy.wait()


def finish(adjoint, outflow, k, v, q_part, k_part, v_part, qg, kg, vg, a_v, o_v, k_v, v_v, kp, vp, sem, out_sem):
    tokens, width = k_v.shape
    size = width // 2
    half = tokens // 2
    through = pltpu.make_async_copy(q_part, qg, out_sem.at[2, 0])
    early = [
        pltpu.make_async_copy(src, dst, sem.at[0, i])
        for i, (src, dst) in enumerate(((adjoint, a_v), (outflow, o_v), (v, v_v), (k, k_v)))
    ]
    parts = []
    for c in range(2):
        at = pl.ds(c * half, half)
        for i, (src, dst) in enumerate(((k_part, kp), (v_part, vp))):
            parts.append(pltpu.make_async_copy(src.at[at], dst.at[at], sem.at[1 + i, c]))
    for copy in early + parts + [through]:
        copy.start()
    for copy in early:
        copy.wait()
    outs = []
    for c in range(2):
        at = slice(c * half, (c + 1) * half)
        rows = pl.ds(c * half, half)
        for i in range(2):
            parts[2 * c + i].wait()
            for h in range(2):
                cols = slice(h * size, (h + 1) * size)
                term = nn(k_v[at, cols], a_v[h]) if i else nt(v_v[at, cols], a_v[h])
                part = vp if i else kp
                part[at, cols] += o_v[at, h : h + 1] * term
            src, dst = (vp, vg) if i else (kp, kg)
            copy = pltpu.make_async_copy(src.at[rows], dst.at[rows], out_sem.at[i, c])
            copy.start()
            outs.append(copy)
    for copy in outs + [through]:
        copy.wait()


def on_device(planes, lines, out_grad, out_proj, query_rows, key_rows, value_rows, log_decay, doc_starts):
    tokens, width = query_rows.shape
    feats = out_grad.shape[1]
    size = width // 2
    chips = planes * lines
    height, wide = size * 2 // chips, size // 2
    any_space = pl.BlockSpec(memory_space=pl.ANY)
    result = jax.ShapeDtypeStruct((tokens, width), F32)
    adjoint = jax.ShapeDtypeStruct((2, size, size), BF16)
    outflow = jax.ShapeDtypeStruct((tokens, 128), F32)
    tile = (8, 128)
    scratch = [
        pltpu.VMEM((4, tokens, feats), BF16),
        pltpu.VMEM((4, width, feats), BF16),
        pltpu.VMEM((tokens, width), BF16),
        pltpu.VMEM((tokens, width), BF16),
        pltpu.VMEM((tokens, width), BF16),
        pltpu.VMEM((tokens, width), F32),
        pltpu.VMEM((tokens, width), BF16),
        pltpu.VMEM((2, tokens, tokens), F32),
        pltpu.VMEM((2, tokens, tokens), BF16),
        pltpu.VMEM((2, tokens, tokens), BF16),
        pltpu.VMEM((tokens, width), BF16),
        pltpu.VMEM((2, tokens, 1), F32),
        pltpu.VMEM((2, tokens, 1), F32),
        pltpu.VMEM((tokens, width), F32),
        pltpu.VMEM((tokens, width), F32),
        pltpu.VMEM((tokens, width), F32),
        pltpu.VMEM((tokens, 128), F32),
        pltpu.VMEM((2,) + tile, F32),
        pltpu.VMEM(tile, F32),
        pltpu.VMEM(tile, F32),
        pltpu.VMEM((chips,) + tile, F32),
        pltpu.VMEM((2, 2, size, size), F32),
        pltpu.VMEM((2, size, size), BF16),
        pltpu.VMEM((2, size, size), BF16),
        pltpu.VMEM((2, chips, height, wide), BF16),
        pltpu.VMEM((2, chips, height, wide), BF16),
        pltpu.VMEM((2, chips, height, wide), BF16),
        pltpu.VMEM((2, chips, height, wide), BF16),
        pltpu.VMEM((2, size, size), BF16),
        pltpu.VMEM((2, 2, size, size), BF16),
        pltpu.SemaphoreType.DMA((8,)),
        pltpu.SemaphoreType.DMA((4, 2)),
        pltpu.SemaphoreType.DMA((3, CHUNKS)),
        pltpu.SemaphoreType.DMA((3, CHUNKS)),
        pltpu.SemaphoreType.DMA((4,)),
        pltpu.SemaphoreType.DMA((2, 4)),
        pltpu.SemaphoreType.DMA((2, 4)),
    ]
    q_part, k_part, v_part, adjoint, outflow = pl.pallas_call(
        functools.partial(kernel, planes, lines),
        out_shape=(result, result, result, adjoint, outflow),
        in_specs=[
            pl.BlockSpec(memory_space=pltpu.SMEM),
            pl.BlockSpec(memory_space=pltpu.VMEM),
        ] + [pl.BlockSpec(memory_space=pltpu.HBM)] * 5,
        out_specs=(any_space,) * 5,
        scratch_shapes=scratch,
        compiler_params=pltpu.CompilerParams(
            collective_id=0, has_side_effects=True, vmem_limit_bytes=32 * 1024 * 1024
        ),
        name="retention_backward",
    )(doc_starts, log_decay, out_grad, out_proj, query_rows, key_rows, value_rows)
    return pl.pallas_call(
        finish,
        out_shape=(result, result, result),
        in_specs=[any_space] * 2 + [pl.BlockSpec(memory_space=pltpu.HBM)] * 2 + [any_space] * 3,
        out_specs=(any_space,) * 3,
        scratch_shapes=[
            pltpu.VMEM((2, size, size), BF16),
            pltpu.VMEM((tokens, 128), F32),
            pltpu.VMEM((tokens, width), BF16),
            pltpu.VMEM((tokens, width), BF16),
            pltpu.VMEM((tokens, width), F32),
            pltpu.VMEM((tokens, width), F32),
            pltpu.SemaphoreType.DMA((3, 4)),
            pltpu.SemaphoreType.DMA((3, 2)),
        ],
        compiler_params=pltpu.CompilerParams(vmem_limit_bytes=16 * 1024 * 1024),
        name="finish",
    )(adjoint, outflow, key_rows, value_rows, q_part, k_part, v_part)


def solution(mesh):
    lines = PLANE
    planes = mesh.shape["ctx"] // (2 * lines)
    return jax.shard_map(
        functools.partial(on_device, planes, lines),
        mesh=mesh,
        in_specs=(
            P("ctx", "head"),
            P("head", None),
            P("ctx", "head"),
            P("ctx", "head"),
            P("ctx", "head"),
            P("head", "ctx"),
            P(),
        ),
        out_specs=(P("ctx", "head"), P("ctx", "head"), P("ctx", "head")),
        check_vma=False,
    )
```

time: 61.6 us -> 63.3 us (1.028)
  local copies, waits for them, and re-layouts: 4.36 us -> 7.28 us
  Pallas kernels: 56.5 us -> 55.1 us
    unnamed x7 -> x14, local copies, waits for them, and re-layouts: 4.36 us -> 7.28 us
    pallas_call x1 -> x2, Pallas kernels: 56.5 us -> 55.1 us  [the longest x1 52.8 us: on_device(): pl.pallas_call(functools.partial(kernel, planes, lines), out_shape=(resul...]
where the time goes in v2:
time: 63.3 us; the launch traced here: 63 us
  Pallas kernels  55.1 us (87%)
  local copies, waits for them, and re-layouts  7.28 us (12%)
  between operations  0.66 us (1%)
    pallas_call x1, Pallas kernels, on_device(): pl.pallas_call(functools.partial(kernel, planes, lines), out_shape=(resul...  52.8 us
    unnamed x14, local copies, waits for them, and re-layouts  7.28 us
    pallas_call x1, Pallas kernels, on_device(): pl.pallas_call(finish, out_shape=(result, result, result), in_specs=[any_...  2.25 us

profile of v2, /device:TPU:1, one launch (start us, length us, event | category | flops | bytes accessed | tf_op | source)
XLA Modules:
  0.0 63.0 jit_solution(10537578795073928310)
XLA Ops:
  0.6 0.0 copy-start
  0.6 1.7 %copy-done = bf16[512,2560]{1,0:T(8,128)(2,1)S(1)} copy-done((bf16[512,2560]{1,0:T(8,128)(2,1)S(1)}, bf16[512,2560]{1,0:T(8,128)(2,1)}, u32[]{:S(2)}) %copy-start) | copy-done | bytes 2621464
  2.4 0.0 copy-start.1
  2.4 1.0 %copy-done.1 = bf16[512,512]{1,0:T(8,128)(2,1)S(1)} copy-done((bf16[512,512]{1,0:T(8,128)(2,1)S(1)}, bf16[512,512]{1,0:T(8,128)(2,1)}, u32[]{:S(2)}) %copy-start.1) | copy-done | bytes 524312
  3.4 0.0 copy-start.2
  3.4 1.0 %copy-done.2 = bf16[512,512]{1,0:T(8,128)(2,1)S(1)} copy-done((bf16[512,512]{1,0:T(8,128)(2,1)S(1)}, bf16[512,512]{1,0:T(8,128)(2,1)}, u32[]{:S(2)}) %copy-start.2) | copy-done | bytes 524312
  4.5 0.0 copy-start.3
  4.5 1.1 %copy-done.3 = bf16[512,640]{1,0:T(8,128)(2,1)S(1)} copy-done((bf16[512,640]{1,0:T(8,128)(2,1)S(1)}, bf16[512,640]{1,0:T(8,128)(2,1)}, u32[]{:S(2)}) %copy-start.3) | copy-done | bytes 655384
  5.5 0.0 copy-start.4
  5.5 1.0 %copy-done.4 = bf16[512,512]{1,0:T(8,128)(2,1)S(1)} copy-done((bf16[512,512]{1,0:T(8,128)(2,1)S(1)}, bf16[512,512]{1,0:T(8,128)(2,1)}, u32[]{:S(2)}) %copy-start.4) | copy-done | bytes 524312
  6.6 0.0 copy-start.5
  6.6 0.7 %copy-done.5 = f32[2,512]{1,0:T(2,128)S(1)} copy-done((f32[2,512]{1,0:T(2,128)S(1)}, f32[2,512]{1,0:T(2,128)}, u32[]{:S(2)}) %copy-start.5) | copy-done | bytes 4120
  7.3 0.0 copy-start.6
  7.3 0.7 %copy-done.6 = s32[3]{0:T(128)S(1)} copy-done((s32[3]{0:T(128)S(1)}, s32[3]{0:T(128)}, u32[]{:S(2)}) %copy-start.6) | copy-done | bytes 36
  7.9 52.8 %retention_backward.1 = (f32[512,512]{1,0:T(8,128)S(1)}, f32[512,512]{1,0:T(8,128)S(1)}, f32[512,512]{1,0:T(8,128)S(1)}, bf16[2,256,256]{2,1,0:T(8,128)(2,1)S(1)}, f32[512,128]{1,0:T(8,128)S(1)}) custom-call(s32[3]{0:T(128)S(1)} %copy-done.6, f32[2,512]{1,0:T(2,128)S(1)} %copy-done.5, bf16[512,640]{1,0:T(8,128)(2,1)S(1)} %copy-done.3, ...), custom_call_target="tpu_custom_call" | custom-call | tf_op jit(solution)/shard_map/retention_backward/pallas_call | solution.py:417
  60.8 2.2 %finish.1 = (f32[512,512]{1,0:T(8,128)}, f32[512,512]{1,0:T(8,128)}, f32[512,512]{1,0:T(8,128)}) custom-call(bf16[2,256,256]{2,1,0:T(8,128)(2,1)S(1)} %get-tuple-element.8.adjoint, f32[512,128]{1,0:T(8,128)S(1)} %get-tuple-element.9.outflow, bf16[512,512]{1,0:T(8,128)(2,1)S(1)} %copy-done.1, bf16[512,512]{1,0:T(8,128)(2,1)S(1)} %copy-done.2, ...), custom_call_target="tpu_custom_call" | custom-call | tf_op jit(solution)/shard_map/finish/pallas_call | solution.py:431
Async XLA Ops:
  0.6 1.7 %copy-start = (bf16[512,2560]{1,0:T(8,128)(2,1)S(1)}, bf16[512,2560]{1,0:T(8,128)(2,1)}, u32[]{:S(2)}) copy-start(bf16[512,2560]{1,0:T(8,128)(2,1)} %w.1) | copy-start | bytes 7864324
  2.4 1.0 %copy-start.1 = (bf16[512,512]{1,0:T(8,128)(2,1)S(1)}, bf16[512,512]{1,0:T(8,128)(2,1)}, u32[]{:S(2)}) copy-start(bf16[512,512]{1,0:T(8,128)(2,1)} %k.3) | copy-start | bytes 1572868
  3.4 1.0 %copy-start.2 = (bf16[512,512]{1,0:T(8,128)(2,1)S(1)}, bf16[512,512]{1,0:T(8,128)(2,1)}, u32[]{:S(2)}) copy-start(bf16[512,512]{1,0:T(8,128)(2,1)} %v.3) | copy-start | bytes 1572868
  4.5 1.1 %copy-start.3 = (bf16[512,640]{1,0:T(8,128)(2,1)S(1)}, bf16[512,640]{1,0:T(8,128)(2,1)}, u32[]{:S(2)}) copy-start(bf16[512,640]{1,0:T(8,128)(2,1)} %og.1) | copy-start | bytes 1966084
  5.5 1.0 %copy-start.4 = (bf16[512,512]{1,0:T(8,128)(2,1)S(1)}, bf16[512,512]{1,0:T(8,128)(2,1)}, u32[]{:S(2)}) copy-start(bf16[512,512]{1,0:T(8,128)(2,1)} %q.1) | copy-start | bytes 1572868
  6.6 0.7 %copy-start.5 = (f32[2,512]{1,0:T(2,128)S(1)}, f32[2,512]{1,0:T(2,128)}, u32[]{:S(2)}) copy-start(f32[2,512]{1,0:T(2,128)} %ld.1) | copy-start | bytes 12292
  7.3 0.7 %copy-start.6 = (s32[3]{0:T(128)S(1)}, s32[3]{0:T(128)}, u32[]{:S(2)}) copy-start(s32[3]{0:T(128)} %doc.1) | copy-start | bytes 40

commit v3 on v2

--- a/solution.py
+++ b/solution.py
@@ -416,22 +416,26 @@
     ]
     q_part, k_part, v_part, adjoint, outflow = pl.pallas_call(
         functools.partial(kernel, planes, lines),
-        out_shape=(result, result, result, adjoint, outflow),
+        out_shape=tuple(pltpu.VMEM(a.shape, a.dtype) for a in (result, result, result, adjoint, outflow)),
         in_specs=[
             pl.BlockSpec(memory_space=pltpu.SMEM),
             pl.BlockSpec(memory_space=pltpu.VMEM),
-        ] + [pl.BlockSpec(memory_space=pltpu.HBM)] * 5,
+        ] + [any_space] * 5,
         out_specs=(any_space,) * 5,
         scratch_shapes=scratch,
         compiler_params=pltpu.CompilerParams(
             collective_id=0, has_side_effects=True, vmem_limit_bytes=32 * 1024 * 1024
         ),
         name="retention_backward",
-    )(doc_starts, log_decay, out_grad, out_proj, query_rows, key_rows, value_rows)
+    )(*(
+        pltpu.with_memory_space_constraint(a, pltpu.HBM)
+        for a in (doc_starts, log_decay, out_grad, out_proj, query_rows, key_rows, value_rows)
+    ))
+    key_rows, value_rows = (pltpu.with_memory_space_constraint(a, pltpu.HBM) for a in (key_rows, value_rows))
     return pl.pallas_call(
         finish,
         out_shape=(result, result, result),
-        in_specs=[any_space] * 2 + [pl.BlockSpec(memory_space=pltpu.HBM)] * 2 + [any_space] * 3,
+        in_specs=[any_space] * 7,
         out_specs=(any_space,) * 3,
         scratch_shapes=[
             pltpu.VMEM((2, size, size), BF16),

time: 63.3 us -> 57 us (0.900)
  local copies, waits for them, and re-layouts: 7.28 us -> 0 us
  Pallas kernels: 55.1 us -> 56.2 us
    unnamed x14 -> x0, local copies, waits for them, and re-layouts: 7.28 us -> none
    pallas_call x1, Pallas kernels: 2.25 us -> 3.6 us  [on_device(): pl.pallas_call(finish, out_shape=(result, result, result), in_specs=[any_...]
where the time goes in v3:
time: 57 us; the launch traced here: 56.8 us
  Pallas kernels  56.2 us (99%)
  between operations  0.64 us (1%)
    pallas_call x1, Pallas kernels, on_device(): pl.pallas_call(functools.partial(kernel, planes, lines), out_shape=tuple(...  52.6 us
    pallas_call x1, Pallas kernels, on_device(): pl.pallas_call(finish, out_shape=(result, result, result), in_specs=[any_...  3.6 us

profile of v3, /device:TPU:1, one launch (start us, length us, event | category | flops | bytes accessed | tf_op | source)
XLA Modules:
  0.0 56.8 jit_solution(9604757623426362162)
XLA Ops:
  0.6 52.6 %retention_backward.1 = (f32[512,512]{1,0:T(8,128)S(1)}, f32[512,512]{1,0:T(8,128)S(1)}, f32[512,512]{1,0:T(8,128)S(1)}, bf16[2,256,256]{2,1,0:T(8,128)(2,1)S(1)}, f32[512,128]{1,0:T(8,128)S(1)}) custom-call(s32[3]{0:T(128)} %doc.1, f32[2,512]{1,0:T(2,128)} %ld.1, bf16[512,640]{1,0:T(8,128)(2,1)} %og.1, bf16[512,2560]{1,0:T(8,128)(2,1)} %w.1, ...), custom_call_target="tpu_custom_call" | custom-call | tf_op jit(solution)/shard_map/retention_backward/pallas_call | solution.py:417
  53.2 3.6 %finish.1 = (f32[512,512]{1,0:T(8,128)}, f32[512,512]{1,0:T(8,128)}, f32[512,512]{1,0:T(8,128)}) custom-call(bf16[2,256,256]{2,1,0:T(8,128)(2,1)S(1)} %get-tuple-element.8.adjoint, f32[512,128]{1,0:T(8,128)S(1)} %get-tuple-element.9.outflow, bf16[512,512]{1,0:T(8,128)(2,1)} %k.3, bf16[512,512]{1,0:T(8,128)(2,1)} %v.3, ...), custom_call_target="tpu_custom_call" | custom-call | tf_op jit(solution)/shard_map/finish/pallas_call | solution.py:435

commit v4 on v3

--- a/solution.py
+++ b/solution.py
@@ -31,14 +31,18 @@
     return half + lax.rem(n + 1, 2) * (n // 2) - lax.rem(n, 2) * ((n + 1) // 2)
 
 
+def ring_offsets(distance, size):
+    return sorted({distance % size, -distance % size} - {0})
+
+
 def kernel(
     planes, lines,
     doc, ld, og, w, q, k, v,
-    qg, kg, vg, adjoint, outflow,
+    qg, kg, vg, adjoint, outflow, k_out, v_out,
     og_v, w_v, q_v, k_v, v_v, acc, g_v, wt, sm, fm, dq, inc, outc, qg_v, kg_v, vg_v, oc_v,
     t_send, t_other, tc_send, t_rec, own, core_send, core_rec, ch_send, ch_rec, en_send, en_rec,
     back_send, st_in,
-    local_sem, out_sem, y_send, y_rec, t_sem, c_send, c_rec,
+    local_sem, out_sem, y_send, y_rec, t_sem, c_send, c_rec, greet_sem,
 ):
     tokens, width = q_v.shape
     feats = og_v.shape[2]
@@ -67,16 +71,26 @@
         there = (z + far_first(n // lines, planes)) % planes
         return there * lines + (x + far_first(n % lines, lines)) % lines
 
+    def at_chip(dz, dx):
+        return (((z + dz) % planes * lines + (x + dx) % lines) * 2 + core, y)
+
+    near_z, far_z = ring_offsets(1, planes), ring_offsets(2, planes)
+    near_x = [at_chip(0, d) for d in ring_offsets(1, lines)]
+    near_z, far_z = [at_chip(d, 0) for d in near_z], [at_chip(d, 0) for d in far_z]
+    rounds = [near_z + near_x, near_z + far_z, far_z]
     barrier = pltpu.get_barrier_semaphore()
-
-    def greet(n, c):
-        pl.semaphore_signal(barrier, inc=1, device_id=(partner(n) * 2 + core, y), device_id_type=MESH)
-        return c
-
-    lax.fori_loop(0, chips - 1, greet, 0)
-    for near in ((ctx, left), (ctx, right), (other, y)):
+    entry = [(ctx, left), (ctx, right), (other, y)] + near_z + near_x
+    for near in entry:
         pl.semaphore_signal(barrier, inc=1, device_id=near, device_id_type=MESH)
-    pl.semaphore_wait(barrier, 3 + chips - 1)
+    pl.semaphore_wait(barrier, len(entry))
+
+    def tell(i):
+        for to in rounds[i]:
+            pl.semaphore_signal(greet_sem.at[i], inc=1, device_id=to, device_id_type=MESH)
+
+    def hear(i):
+        if rounds[i]:
+            pl.semaphore_wait(greet_sem.at[i], len(rounds[i]))
 
     def hop(src_slot, dst_slot, c, to, lane):
         at = pl.ds(c * chunk, chunk)
@@ -93,6 +107,7 @@
     for c in range(CHUNKS):
         to_right[c].start()
         to_left[CHUNKS - 1 - c].start()
+    tell(0)
 
     offset = ctx * tokens
     lane = lax.broadcasted_iota(jnp.int32, (8, tokens), 1)
@@ -229,25 +244,30 @@
         decayed = (k_v[:, cols(h)].astype(F32) * outc[h]).astype(BF16)
         own[0, h] = tn(decayed, v_v[:, cols(h)])
     first_send(0)
+    hear(0)
+    tell(1)
+
+    loads[3].wait()
+    q_v[...] = q_v[...] * jnp.asarray(factor, BF16)
+    at_lane = lax.broadcasted_iota(jnp.int32, oc_v.shape, 1)
+    oc_v[...] = jnp.where(at_lane == 0, outc[0], outc[1])
+    for h in range(2):
+        dq[:, cols(h)] = (q_v[:, cols(h)].astype(F32) * inc[h]).astype(BF16)
+        cum_row, cum_col = cums[h]
+        wt[h] = jnp.exp(jnp.where(same, cum_col - cum_row, -1e30))
+        sm[h] = (nt(q_v[:, cols(h)], k_v[:, cols(h)]) * wt[h]).astype(BF16)
+    hear(1)
+    tell(2)
+    loads[4].wait()
+    acc[...] = nt(og_v[0], w_v[0])
+    for i in range(1, 4):
+        loads[4 + i].wait()
+    hear(2)
     t_copy.wait_recv()
     tc_send[...] = t_send[core] * t_other[...]
     to_chips(tc_send, t_rec, t_sem.at[2], t_sem.at[3], lambda j: slice(None))
     t_rec[chip] = tc_send[...]
     second_send(0)
-
-    loads[3].wait()
-    q_v[...] = q_v[...] * jnp.asarray(factor, BF16)
-    at_lane = lax.broadcasted_iota(jnp.int32, oc_v.shape, 1)
-    oc_v[...] = jnp.where(at_lane == 0, outc[0], outc[1])
-    for h in range(2):
-        dq[:, cols(h)] = (q_v[:, cols(h)].astype(F32) * inc[h]).astype(BF16)
-        cum_row, cum_col = cums[h]
-        wt[h] = jnp.exp(jnp.where(same, cum_col - cum_row, -1e30))
-        sm[h] = (nt(q_v[:, cols(h)], k_v[:, cols(h)]) * wt[h]).astype(BF16)
-    loads[4].wait()
-    acc[...] = nt(og_v[0], w_v[0])
-    for i in range(1, 4):
-        loads[4 + i].wait()
 
     def add(slot, c):
         at = slice(c * chunk, (c + 1) * chunk)
@@ -261,16 +281,13 @@
         onward[CHUNKS - 1 - c].start()
         add(1, c)
         add(2, CHUNKS - 1 - c)
-        if c == 0:
-            arrived(t_rec, chips - 1, t_sem.at[3])
-            third_send(0)
     for c in range(half):
         to_right[half + c].wait_recv()
         add(1, half + c)
         to_left[half - 1 - c].wait_recv()
         add(2, half - 1 - c)
-        if c == 0:
-            fourth_send(0)
+    arrived(t_rec, chips - 1, t_sem.at[3])
+    third_send(0)
 
     adj = [jnp.zeros((size, size), F32), jnp.zeros((size, size), F32)]
     for c in range(half):
@@ -284,9 +301,13 @@
     for h in range(2):
         own[1, h] = adj[h]
     first_send(1)
+    fourth_send(0)
 
     outs = [pltpu.make_async_copy(oc_v, outflow, out_sem.at[3, 0])]
-    outs[0].start()
+    for i, (src, dst) in enumerate(((k_v, k_out), (v_v, v_out))):
+        outs.append(pltpu.make_async_copy(src, dst, out_sem.at[4, i]))
+    for copy in outs:
+        copy.start()
 
     def put(src, dst, h, i):
         copy = pltpu.make_async_copy(src.at[:, cols(h)], dst.at[:, cols(h)], out_sem.at[i, h])
@@ -327,40 +348,24 @@
     last_copy.wait()
 
 
-def finish(adjoint, outflow, k, v, q_part, k_part, v_part, qg, kg, vg, a_v, o_v, k_v, v_v, kp, vp, sem, out_sem):
-    tokens, width = k_v.shape
+def finish(adjoint, outflow, k, v, k_part, v_part, q_part, qg, kg, vg, k_all, v_all, sem):
+    tokens, width = k.shape
     size = width // 2
-    half = tokens // 2
-    through = pltpu.make_async_copy(q_part, qg, out_sem.at[2, 0])
-    early = [
-        pltpu.make_async_copy(src, dst, sem.at[0, i])
-        for i, (src, dst) in enumerate(((adjoint, a_v), (outflow, o_v), (v, v_v), (k, k_v)))
-    ]
-    parts = []
-    for c in range(2):
-        at = pl.ds(c * half, half)
-        for i, (src, dst) in enumerate(((k_part, kp), (v_part, vp))):
-            parts.append(pltpu.make_async_copy(src.at[at], dst.at[at], sem.at[1 + i, c]))
-    for copy in early + parts + [through]:
-        copy.start()
-    for copy in early:
-        copy.wait()
-    outs = []
-    for c in range(2):
-        at = slice(c * half, (c + 1) * half)
-        rows = pl.ds(c * half, half)
-        for i in range(2):
-            parts[2 * c + i].wait()
+    step = tokens // 4
+    outs = [pltpu.make_async_copy(q_part, qg, sem.at[2, 0])]
+    outs[0].start()
+    for c in range(4):
+        at = slice(c * step, (c + 1) * step)
+        rows = pl.ds(c * step, step)
+        for i, (part, whole, out) in enumerate(((k_part, k_all, kg), (v_part, v_all, vg))):
             for h in range(2):
                 cols = slice(h * size, (h + 1) * size)
-                term = nn(k_v[at, cols], a_v[h]) if i else nt(v_v[at, cols], a_v[h])
-                part = vp if i else kp
-                part[at, cols] += o_v[at, h : h + 1] * term
-            src, dst = (vp, vg) if i else (kp, kg)
-            copy = pltpu.make_async_copy(src.at[rows], dst.at[rows], out_sem.at[i, c])
+                term = nn(k[at, cols], adjoint[h]) if i else nt(v[at, cols], adjoint[h])
+                whole[at, cols] = part[at, cols] + outflow[at, h : h + 1] * term
+            copy = pltpu.make_async_copy(whole.at[rows], out.at[rows], sem.at[i, c])
             copy.start()
             outs.append(copy)
-    for copy in outs + [through]:
+    for copy in outs:
         copy.wait()
 
 
@@ -407,21 +412,22 @@
         pltpu.VMEM((2, size, size), BF16),
         pltpu.VMEM((2, 2, size, size), BF16),
         pltpu.SemaphoreType.DMA((8,)),
-        pltpu.SemaphoreType.DMA((4, 2)),
+        pltpu.SemaphoreType.DMA((5, 2)),
         pltpu.SemaphoreType.DMA((3, CHUNKS)),
         pltpu.SemaphoreType.DMA((3, CHUNKS)),
         pltpu.SemaphoreType.DMA((4,)),
         pltpu.SemaphoreType.DMA((2, 4)),
         pltpu.SemaphoreType.DMA((2, 4)),
+        pltpu.SemaphoreType.REGULAR((3,)),
     ]
-    q_part, k_part, v_part, adjoint, outflow = pl.pallas_call(
+    q_part, k_part, v_part, adjoint, outflow, key_rows, value_rows = pl.pallas_call(
         functools.partial(kernel, planes, lines),
-        out_shape=tuple(pltpu.VMEM(a.shape, a.dtype) for a in (result, result, result, adjoint, outflow)),
+        out_shape=tuple(pltpu.VMEM(a.shape, a.dtype) for a in (result, result, result, adjoint, outflow, key_rows, value_rows)),
         in_specs=[
             pl.BlockSpec(memory_space=pltpu.SMEM),
             pl.BlockSpec(memory_space=pltpu.VMEM),
         ] + [any_space] * 5,
-        out_specs=(any_space,) * 5,
+        out_specs=(any_space,) * 7,
         scratch_shapes=scratch,
         compiler_params=pltpu.CompilerParams(
             collective_id=0, has_side_effects=True, vmem_limit_bytes=32 * 1024 * 1024
@@ -431,25 +437,19 @@
         pltpu.with_memory_space_constraint(a, pltpu.HBM)
         for a in (doc_starts, log_decay, out_grad, out_proj, query_rows, key_rows, value_rows)
     ))
-    key_rows, value_rows = (pltpu.with_memory_space_constraint(a, pltpu.HBM) for a in (key_rows, value_rows))
     return pl.pallas_call(
         finish,
         out_shape=(result, result, result),
-        in_specs=[any_space] * 7,
+        in_specs=[pl.BlockSpec(memory_space=pltpu.VMEM)] * 6 + [any_space],
         out_specs=(any_space,) * 3,
         scratch_shapes=[
-            pltpu.VMEM((2, size, size), BF16),
-            pltpu.VMEM((tokens, 128), F32),
-            pltpu.VMEM((tokens, width), BF16),
-            pltpu.VMEM((tokens, width), BF16),
             pltpu.VMEM((tokens, width), F32),
             pltpu.VMEM((tokens, width), F32),
             pltpu.SemaphoreType.DMA((3, 4)),
-            pltpu.SemaphoreType.DMA((3, 2)),
         ],
         compiler_params=pltpu.CompilerParams(vmem_limit_bytes=16 * 1024 * 1024),
         name="finish",
-    )(adjoint, outflow, key_rows, value_rows, q_part, k_part, v_part)
+    )(adjoint, outflow, key_rows, value_rows, k_part, v_part, q_part)
 
 
 def solution(mesh):

time: 57 us -> 52.3 us (0.918)
  Pallas kernels: 56.2 us -> 51.5 us
    pallas_call x1, Pallas kernels: 52.6 us -> 49.8 us  [on_device(): pl.pallas_call(functools.partial(kernel, planes, lines), out_shape=tuple(...]
    pallas_call x1, Pallas kernels: 3.6 us -> 1.77 us  [on_device(): pl.pallas_call(finish, out_shape=(result, result, result), in_specs=[pl.B...]
where the time goes in v4:
time: 52.3 us; the launch traced here: 52.2 us
  Pallas kernels  51.5 us (98%)
  between operations  0.64 us (1%)
    pallas_call x1, Pallas kernels, on_device(): pl.pallas_call(functools.partial(kernel, planes, lines), out_shape=tuple(...  49.8 us
    pallas_call x1, Pallas kernels, on_device(): pl.pallas_call(finish, out_shape=(result, result, result), in_specs=[pl.B...  1.77 us

profile of v4, /device:TPU:1, one launch (start us, length us, event | category | flops | bytes accessed | tf_op | source)
XLA Modules:
  0.0 52.2 jit_solution(8877015777012651976)
XLA Ops:
  0.6 49.8 %retention_backward.1 = (f32[512,512]{1,0:T(8,128)S(1)}, f32[512,512]{1,0:T(8,128)S(1)}, f32[512,512]{1,0:T(8,128)S(1)}, bf16[2,256,256]{2,1,0:T(8,128)(2,1)S(1)...) custom-call(s32[3]{0:T(128)} %doc.1, f32[2,512]{1,0:T(2,128)} %ld.1, ...), custom_call_target="tpu_custom_call" | custom-call | tf_op jit(solution)/shard_map/retention_backward/pallas_call | solution.py:423
  50.4 1.8 %finish.1 = (f32[512,512]{1,0:T(8,128)}, f32[512,512]{1,0:T(8,128)}, f32[512,512]{1,0:T(8,128)}) custom-call(bf16[2,256,256]{2,1,0:T(8,128)(2,1)S(1)} %get-tuple-element.10.adjoint, f32[512,128]{1,0:T(8,128)S(1)} %get-tuple-element.11.outflow, bf16[512,512]{1,0:T(8,128)(2,1)S(1)} %get-tuple-element.12.k, bf16[512,512]{1,0:T(8,128)(2,1)S(1)} %get-tuple-element.13.v, ...), custom_call_target="tpu_custom_call" | custom-call | tf_op jit(solution)/shard_map/finish/pallas_call | solution.py:440

commit v5 on v4

--- a/solution.py
+++ b/solution.py
@@ -37,11 +37,11 @@
 
 def kernel(
     planes, lines,
-    doc, ld, og, w, q, k, v,
+    doc_in, ld_in, og, w, q, k, v,
     qg, kg, vg, adjoint, outflow, k_out, v_out,
-    og_v, w_v, q_v, k_v, v_v, acc, g_v, wt, sm, fm, dq, inc, outc, qg_v, kg_v, vg_v, oc_v,
+    doc, ld, og_v, w_v, q_v, k_v, v_v, acc, g_v, wt, sm, fm, dq, inc, outc, qg_v, kg_v, vg_v, oc_v,
     t_send, t_other, tc_send, t_rec, own, core_send, core_rec, ch_send, ch_rec, en_send, en_rec,
-    back_send, st_in,
+    back_send, back_rec, state,
     local_sem, out_sem, y_send, y_rec, t_sem, c_send, c_rec, greet_sem,
 ):
     tokens, width = q_v.shape
@@ -58,19 +58,6 @@
     right, left = (y + 1) % 4, (y + 3) % 4
     owners = (y, left, right, (y + 2) % 4)
 
-    loads = [pltpu.make_async_copy(og, og_v.at[0], local_sem.at[0])]
-    for i, (src, dst) in enumerate(((k, k_v), (v, v_v), (q, q_v))):
-        loads.append(pltpu.make_async_copy(src, dst, local_sem.at[1 + i]))
-    for i in range(4):
-        start = pl.multiple_of(owners[i] * feats, 128)
-        loads.append(pltpu.make_async_copy(w.at[:, pl.ds(start, feats)], w_v.at[i], local_sem.at[4 + i]))
-    for load in loads:
-        load.start()
-
-    def partner(n):
-        there = (z + far_first(n // lines, planes)) % planes
-        return there * lines + (x + far_first(n % lines, lines)) % lines
-
     def at_chip(dz, dx):
         return (((z + dz) % planes * lines + (x + dx) % lines) * 2 + core, y)
 
@@ -82,6 +69,15 @@
     entry = [(ctx, left), (ctx, right), (other, y)] + near_z + near_x
     for near in entry:
         pl.semaphore_signal(barrier, inc=1, device_id=near, device_id_type=MESH)
+    loads = [pltpu.make_async_copy(og, og_v.at[0], local_sem.at[0])]
+    for i, (src, dst) in enumerate(((k, k_v), (v, v_v), (q, q_v))):
+        loads.append(pltpu.make_async_copy(src, dst, local_sem.at[1 + i]))
+    for i in range(4):
+        start = pl.multiple_of(owners[i] * feats, 128)
+        loads.append(pltpu.make_async_copy(w.at[:, pl.ds(start, feats)], w_v.at[i], local_sem.at[4 + i]))
+    small = [pltpu.make_async_copy(ld_in, ld, local_sem.at[8]), pltpu.make_async_copy(doc_in, doc, local_sem.at[9])]
+    for load in small + loads:
+        load.start()
     pl.semaphore_wait(barrier, len(entry))
 
     def tell(i):
@@ -111,6 +107,8 @@
 
     offset = ctx * tokens
     lane = lax.broadcasted_iota(jnp.int32, (8, tokens), 1)
+    for load in small:
+        load.wait()
     docs = [doc[i] for i in range(doc.shape[0])]
 
     def segment(places):
@@ -155,16 +153,28 @@
             device_id=(other, y), device_id_type=MESH,
         )
 
+    columns = sorted(range(lines), key=lambda d: -min(d, lines - d))
+    columns = [(x + d) % lines for d in columns]
+
     def to_chips(src, dst, send, recv, index):
-        def one(n, c):
-            j = partner(n)
+        def one(j):
             pltpu.make_async_remote_copy(
                 src_ref=src.at[index(j)], dst_ref=dst.at[chip], send_sem=send, recv_sem=recv,
                 device_id=(j * 2 + core, y), device_id_type=MESH,
             ).start()
+
+        def row(n, c):
+            there = (z + far_first(n, planes)) % planes * lines
+            for line in columns[:-1]:
+                one(there + line)
+
+            @pl.when(n < planes - 1)
+            def _():
+                one(there + columns[-1])
+
             return c
 
-        lax.fori_loop(0, chips - 1, one, 0)
+        lax.fori_loop(0, planes, row, 0)
 
     def arrived(ref, count, sem):
         part = ref.at[pl.ds(0, count)]
@@ -183,7 +193,7 @@
 
     def back_copy(direction):
         return to_core(
-            back_send.at[direction], st_in.at[direction, core], c_send.at[direction, 3], c_rec.at[direction, 3]
+            back_send.at[direction], adjoint if direction else back_rec, c_send.at[direction, 3], c_rec.at[direction, 3]
         )
 
     def first_send(direction):
@@ -233,7 +243,7 @@
         back_send[direction] = (a * entering + b * own[direction, core]).astype(BF16)
         back_copy(direction).start()
         a = jnp.where(earlier, 1.0, decay(t_other))
-        st_in[direction, core] = (a * entering + (1.0 - b) * core_rec[direction].astype(F32)).astype(BF16)
+        return (a * entering + (1.0 - b) * core_rec[direction].astype(F32)).astype(BF16)
 
     def cols(h):
         return slice(h * size, (h + 1) * size)
@@ -286,22 +296,24 @@
         add(1, half + c)
         to_left[half - 1 - c].wait_recv()
         add(2, half - 1 - c)
-    arrived(t_rec, chips - 1, t_sem.at[3])
-    third_send(0)
-
-    adj = [jnp.zeros((size, size), F32), jnp.zeros((size, size), F32)]
+
+    heads = (1 - core, core)
+    for h in range(2):
+        own[1, h] = jnp.zeros((size, size), F32)
     for c in range(half):
         for at in (c, CHUNKS - 1 - c):
             onward[at].wait_recv()
             span = slice(at * chunk, (at + 1) * chunk)
-            here = (acc[span, :] + nt(og_v[3, span], w_v[3])).astype(BF16)
-            g_v[span, :] = here
-            for h in range(2):
-                adj[h] = adj[h] + tn(dq[span, cols(h)], here[:, cols(h)])
-    for h in range(2):
-        own[1, h] = adj[h]
-    first_send(1)
-    fourth_send(0)
+            g_v[span, :] = (acc[span, :] + nt(og_v[3, span], w_v[3])).astype(BF16)
+        for i in range(2):
+            at = pl.ds(pl.multiple_of(heads[i] * size, 128), size)
+            total = own[1, heads[i]]
+            for r in (c, CHUNKS - 1 - c):
+                span = slice(r * chunk, (r + 1) * chunk)
+                total = total + tn(dq[span, at], g_v[span, at])
+            own[1, heads[i]] = total
+            if c == half - 1 and i == 0:
+                first_send(1)
 
     outs = [pltpu.make_async_copy(oc_v, outflow, out_sem.at[3, 0])]
     for i, (src, dst) in enumerate(((k_v, k_out), (v_v, v_out))):
@@ -314,20 +326,22 @@
         copy.start()
         outs.append(copy)
 
+    for h in range(2):
+        fm[h] = (nt(g_v[:, cols(h)], v_v[:, cols(h)]) * wt[h]).astype(BF16)
     second_send(1)
-    for h in range(2):
-        fm[h] = (nt(g_v[:, cols(h)], v_v[:, cols(h)]) * wt[h]).astype(BF16)
+    arrived(t_rec, chips - 1, t_sem.at[3])
+    third_send(0)
+    for h in range(2):
+        kg_v[:, cols(h)] = tn(fm[h], q_v[:, cols(h)])
+        vg_v[:, cols(h)] = tn(sm[h], g_v[:, cols(h)])
+    third_send(1)
+    state[core] = fourth_send(0)
     back_copy(0).wait_recv()
-    for h in range(2):
-        entering = nt(g_v[:, cols(h)], st_in[0, h])
+    state[1 - core] = back_rec[...]
+    for h in range(2):
+        entering = nt(g_v[:, cols(h)], state[h])
         qg_v[:, cols(h)] = factor * (nn(fm[h], k_v[:, cols(h)]) + inc[h] * entering)
         put(qg_v, qg, h, 0)
-    third_send(1)
-    for h in range(2):
-        kg_v[:, cols(h)] = tn(fm[h], q_v[:, cols(h)])
-        put(kg_v, kg, h, 1)
-        vg_v[:, cols(h)] = tn(sm[h], g_v[:, cols(h)])
-        put(vg_v, vg, h, 2)
 
     for copy in to_right + to_left + onward + [t_copy]:
         copy.wait_send()
@@ -338,31 +352,43 @@
     arrived(en_send.at[0], chips - 1, c_send.at[0, 2])
     back_copy(0).wait_send()
 
-    fourth_send(1)
+    mine, theirs = pl.ds(pl.multiple_of(core * size, 128), size), pl.ds(pl.multiple_of(size - core * size, 128), size)
+    for i, (src, dst) in enumerate(((kg_v, kg), (vg_v, vg))):
+        outs.append(pltpu.make_async_copy(src.at[:, theirs], dst.at[:, theirs], out_sem.at[1 + i, 0]))
+        outs[-1].start()
+    entering = fourth_send(1)
+    kg_v[:, mine] += outc[core] * nt(v_v[:, mine], entering)
+    vg_v[:, mine] += outc[core] * nn(k_v[:, mine], entering)
+    for i, (src, dst) in enumerate(((kg_v, kg), (vg_v, vg))):
+        outs.append(pltpu.make_async_copy(src.at[:, mine], dst.at[:, mine], out_sem.at[1 + i, 1]))
+        outs[-1].start()
     arrived(en_send.at[1], chips - 1, c_send.at[1, 2])
     for copy in outs:
         copy.wait()
     back_copy(1).wait()
-    last_copy = pltpu.make_async_copy(st_in.at[1], adjoint, out_sem.at[3, 1])
-    last_copy.start()
-    last_copy.wait()
 
 
 def finish(adjoint, outflow, k, v, k_part, v_part, q_part, qg, kg, vg, k_all, v_all, sem):
     tokens, width = k.shape
     size = width // 2
     step = tokens // 4
-    outs = [pltpu.make_async_copy(q_part, qg, sem.at[2, 0])]
-    outs[0].start()
+    core = lax.axis_index("ctx") % 2
+    done, left = pl.ds(pl.multiple_of(core * size, 128), size), pl.ds(pl.multiple_of(size - core * size, 128), size)
+    outs = [
+        pltpu.make_async_copy(q_part, qg, sem.at[2, 0]),
+        pltpu.make_async_copy(k_part.at[:, done], kg.at[:, done], sem.at[2, 1]),
+        pltpu.make_async_copy(v_part.at[:, done], vg.at[:, done], sem.at[2, 2]),
+    ]
+    for copy in outs:
+        copy.start()
     for c in range(4):
         at = slice(c * step, (c + 1) * step)
         rows = pl.ds(c * step, step)
+        flow = jnp.where(core == 0, outflow[at, 1:2], outflow[at, 0:1])
         for i, (part, whole, out) in enumerate(((k_part, k_all, kg), (v_part, v_all, vg))):
-            for h in range(2):
-                cols = slice(h * size, (h + 1) * size)
-                term = nn(k[at, cols], adjoint[h]) if i else nt(v[at, cols], adjoint[h])
-                whole[at, cols] = part[at, cols] + outflow[at, h : h + 1] * term
-            copy = pltpu.make_async_copy(whole.at[rows], out.at[rows], sem.at[i, c])
+            term = nn(k[at, left], adjoint[...]) if i else nt(v[at, left], adjoint[...])
+            whole[at, :] = part[at, left] + flow * term
+            copy = pltpu.make_async_copy(whole.at[rows], out.at[rows, left], sem.at[i, c])
             copy.start()
             outs.append(copy)
     for copy in outs:
@@ -377,10 +403,12 @@
     height, wide = size * 2 // chips, size // 2
     any_space = pl.BlockSpec(memory_space=pl.ANY)
     result = jax.ShapeDtypeStruct((tokens, width), F32)
-    adjoint = jax.ShapeDtypeStruct((2, size, size), BF16)
+    adjoint = jax.ShapeDtypeStruct((size, size), BF16)
     outflow = jax.ShapeDtypeStruct((tokens, 128), F32)
     tile = (8, 128)
     scratch = [
+        pltpu.SMEM(doc_starts.shape, doc_starts.dtype),
+        pltpu.VMEM(log_decay.shape, F32),
         pltpu.VMEM((4, tokens, feats), BF16),
         pltpu.VMEM((4, width, feats), BF16),
         pltpu.VMEM((tokens, width), BF16),
@@ -410,8 +438,9 @@
         pltpu.VMEM((2, chips, height, wide), BF16),
         pltpu.VMEM((2, chips, height, wide), BF16),
         pltpu.VMEM((2, size, size), BF16),
-        pltpu.VMEM((2, 2, size, size), BF16),
-        pltpu.SemaphoreType.DMA((8,)),
+        pltpu.VMEM((size, size), BF16),
+        pltpu.VMEM((2, size, size), BF16),
+        pltpu.SemaphoreType.DMA((10,)),
         pltpu.SemaphoreType.DMA((5, 2)),
         pltpu.SemaphoreType.DMA((3, CHUNKS)),
         pltpu.SemaphoreType.DMA((3, CHUNKS)),
@@ -423,10 +452,7 @@
     q_part, k_part, v_part, adjoint, outflow, key_rows, value_rows = pl.pallas_call(
         functools.partial(kernel, planes, lines),
         out_shape=tuple(pltpu.VMEM(a.shape, a.dtype) for a in (result, result, result, adjoint, outflow, key_rows, value_rows)),
-        in_specs=[
-            pl.BlockSpec(memory_space=pltpu.SMEM),
-            pl.BlockSpec(memory_space=pltpu.VMEM),
-        ] + [any_space] * 5,
+        in_specs=[any_space] * 7,
         out_specs=(any_space,) * 7,
         scratch_shapes=scratch,
         compiler_params=pltpu.CompilerParams(
@@ -443,8 +469,8 @@
         in_specs=[pl.BlockSpec(memory_space=pltpu.VMEM)] * 6 + [any_space],
         out_specs=(any_space,) * 3,
         scratch_shapes=[
-            pltpu.VMEM((tokens, width), F32),
-            pltpu.VMEM((tokens, width), F32),
+            pltpu.VMEM((tokens, size), F32),
+            pltpu.VMEM((tokens, size), F32),
             pltpu.SemaphoreType.DMA((3, 4)),
         ],
         compiler_params=pltpu.CompilerParams(vmem_limit_bytes=16 * 1024 * 1024),

time: 52.3 us -> 51.7 us (0.989)
    pallas_call x1, Pallas kernels: 49.8 us -> 49.3 us  [on_device(): pl.pallas_call(functools.partial(kernel, planes, lines), out_shape=tuple(...]
where the time goes in v5:
time: 51.7 us; the launch traced here: 51.6 us
  Pallas kernels  51 us (99%)
  between operations  0.64 us (1%)
    pallas_call x1, Pallas kernels, on_device(): pl.pallas_call(functools.partial(kernel, planes, lines), out_shape=tuple(...  49.3 us
    pallas_call x1, Pallas kernels, on_device(): pl.pallas_call(finish, out_shape=(result, result, result), in_specs=[pl.B...  1.75 us

profile of v5, /device:TPU:1, one launch (start us, length us, event | category | flops | bytes accessed | tf_op | source)
XLA Modules:
  0.0 51.6 jit_solution(15218008748745519827)
XLA Ops:
  0.6 49.3 %retention_backward.1 = (f32[512,512]{1,0:T(8,128)S(1)}, f32[512,512]{1,0:T(8,128)S(1)}, f32[512,512]{1,0:T(8,128)S(1)}, bf16[256,256]{1,0:T(8,128)(2,1)S(1)}, f...) custom-call(s32[3]{0:T(128)} %doc_in.1, f32[2,512]{1,0:T(2,128)} %ld_in.1, ...), custom_call_target="tpu_custom_call" | custom-call | tf_op jit(solution)/shard_map/retention_backward/pallas_call | solution.py:452
  49.9 1.8 %finish.1 = (f32[512,512]{1,0:T(8,128)}, f32[512,512]{1,0:T(8,128)}, f32[512,512]{1,0:T(8,128)}) custom-call(bf16[256,256]{1,0:T(8,128)(2,1)S(1)} %get-tuple-element.10.adjoint, f32[512,128]{1,0:T(8,128)S(1)} %get-tuple-element.11.outflow, bf16[512,512]{1,0:T(8,128)(2,1)S(1)} %get-tuple-element.12.k, bf16[512,512]{1,0:T(8,128)(2,1)S(1)} %get-tuple-element.13.v, ...), custom_call_target="tpu_custom_call" | custom-call | tf_op jit(solution)/shard_map/finish/pallas_call | solution.py:466

commit v6 on v5

--- a/solution.py
+++ b/solution.py
@@ -39,7 +39,7 @@
     planes, lines,
     doc_in, ld_in, og, w, q, k, v,
     qg, kg, vg, adjoint, outflow, k_out, v_out,
-    doc, ld, og_v, w_v, q_v, k_v, v_v, acc, g_v, wt, sm, fm, dq, inc, outc, qg_v, kg_v, vg_v, oc_v,
+    doc, ld, og_v, w_v, w_t, q_v, k_v, v_v, acc, g_v, wt, sm, fm, dq, inc, outc, qg_v, kg_v, vg_v, oc_v,
     t_send, t_other, tc_send, t_rec, own, core_send, core_rec, ch_send, ch_rec, en_send, en_rec,
     back_send, back_rec, state,
     local_sem, out_sem, y_send, y_rec, t_sem, c_send, c_rec, greet_sem,
@@ -262,7 +262,7 @@
     at_lane = lax.broadcasted_iota(jnp.int32, oc_v.shape, 1)
     oc_v[...] = jnp.where(at_lane == 0, outc[0], outc[1])
     for h in range(2):
-        dq[:, cols(h)] = (q_v[:, cols(h)].astype(F32) * inc[h]).astype(BF16)
+        dq[h] = (q_v[:, cols(h)].astype(F32) * inc[h]).astype(BF16).T
         cum_row, cum_col = cums[h]
         wt[h] = jnp.exp(jnp.where(same, cum_col - cum_row, -1e30))
         sm[h] = (nt(q_v[:, cols(h)], k_v[:, cols(h)]) * wt[h]).astype(BF16)
@@ -272,6 +272,7 @@
     acc[...] = nt(og_v[0], w_v[0])
     for i in range(1, 4):
         loads[4 + i].wait()
+        w_t[i - 1] = w_v[i].T
     hear(2)
     t_copy.wait_recv()
     tc_send[...] = t_send[core] * t_other[...]
@@ -281,7 +282,7 @@
 
     def add(slot, c):
         at = slice(c * chunk, (c + 1) * chunk)
-        acc[at, :] += nt(og_v[slot, at], w_v[slot])
+        acc[at, :] += nn(og_v[slot, at], w_t[slot - 1])
 
     half = CHUNKS // 2
     for c in range(half):
@@ -304,13 +305,13 @@
         for at in (c, CHUNKS - 1 - c):
             onward[at].wait_recv()
             span = slice(at * chunk, (at + 1) * chunk)
-            g_v[span, :] = (acc[span, :] + nt(og_v[3, span], w_v[3])).astype(BF16)
+            g_v[span, :] = (acc[span, :] + nn(og_v[3, span], w_t[2])).astype(BF16)
         for i in range(2):
             at = pl.ds(pl.multiple_of(heads[i] * size, 128), size)
             total = own[1, heads[i]]
             for r in (c, CHUNKS - 1 - c):
                 span = slice(r * chunk, (r + 1) * chunk)
-                total = total + tn(dq[span, at], g_v[span, at])
+                total = total + nn(dq[heads[i], :, span], g_v[span, at])
             own[1, heads[i]] = total
             if c == half - 1 and i == 0:
                 first_send(1)
@@ -326,9 +327,9 @@
         copy.start()
         outs.append(copy)
 
+    second_send(1)
     for h in range(2):
         fm[h] = (nt(g_v[:, cols(h)], v_v[:, cols(h)]) * wt[h]).astype(BF16)
-    second_send(1)
     arrived(t_rec, chips - 1, t_sem.at[3])
     third_send(0)
     for h in range(2):
@@ -371,7 +372,7 @@
 def finish(adjoint, outflow, k, v, k_part, v_part, q_part, qg, kg, vg, k_all, v_all, sem):
     tokens, width = k.shape
     size = width // 2
-    step = tokens // 4
+    step = tokens // 2
     core = lax.axis_index("ctx") % 2
     done, left = pl.ds(pl.multiple_of(core * size, 128), size), pl.ds(pl.multiple_of(size - core * size, 128), size)
     outs = [
@@ -381,7 +382,7 @@
     ]
     for copy in outs:
         copy.start()
-    for c in range(4):
+    for c in range(2):
         at = slice(c * step, (c + 1) * step)
         rows = pl.ds(c * step, step)
         flow = jnp.where(core == 0, outflow[at, 1:2], outflow[at, 0:1])
@@ -411,6 +412,7 @@
         pltpu.VMEM(log_decay.shape, F32),
         pltpu.VMEM((4, tokens, feats), BF16),
         pltpu.VMEM((4, width, feats), BF16),
+        pltpu.VMEM((3, feats, width), BF16),
         pltpu.VMEM((tokens, width), BF16),
         pltpu.VMEM((tokens, width), BF16),
         pltpu.VMEM((tokens, width), BF16),
@@ -419,7 +421,7 @@
         pltpu.VMEM((2, tokens, tokens), F32),
         pltpu.VMEM((2, tokens, tokens), BF16),
         pltpu.VMEM((2, tokens, tokens), BF16),
-        pltpu.VMEM((tokens, width), BF16),
+        pltpu.VMEM((2, size, tokens), BF16),
         pltpu.VMEM((2, tokens, 1), F32),
         pltpu.VMEM((2, tokens, 1), F32),
         pltpu.VMEM((tokens, width), F32),

time: 51.7 us -> 51.2 us (level)
    pallas_call x1, Pallas kernels: 49.3 us -> 48.7 us  [on_device(): pl.pallas_call(functools.partial(kernel, planes, lines), out_shape=tuple(...]
where the time goes in v6:
time: 51.2 us; the launch traced here: 51.1 us
  Pallas kernels  50.5 us (99%)
  between operations  0.64 us (1%)
    pallas_call x1, Pallas kernels, on_device(): pl.pallas_call(functools.partial(kernel, planes, lines), out_shape=tuple(...  48.7 us
    pallas_call x1, Pallas kernels, on_device(): pl.pallas_call(finish, out_shape=(result, result, result), in_specs=[pl.B...  1.77 us

profile of v6, /device:TPU:1, one launch (start us, length us, event | category | flops | bytes accessed | tf_op | source)
XLA Modules:
  0.0 51.1 jit_solution(6291386727601190220)
XLA Ops:
  0.6 48.7 %retention_backward.1 = (f32[512,512]{1,0:T(8,128)S(1)}, f32[512,512]{1,0:T(8,128)S(1)}, f32[512,512]{1,0:T(8,128)S(1)}, bf16[256,256]{1,0:T(8,128)(2,1)S(1)}, f...) custom-call(s32[3]{0:T(128)} %doc_in.1, f32[2,512]{1,0:T(2,128)} %ld_in.1, ...), custom_call_target="tpu_custom_call" | custom-call | tf_op jit(solution)/shard_map/retention_backward/pallas_call | solution.py:454
  49.4 1.8 %finish.1 = (f32[512,512]{1,0:T(8,128)}, f32[512,512]{1,0:T(8,128)}, f32[512,512]{1,0:T(8,128)}) custom-call(bf16[256,256]{1,0:T(8,128)(2,1)S(1)} %get-tuple-element.10.adjoint, f32[512,128]{1,0:T(8,128)S(1)} %get-tuple-element.11.outflow, bf16[512,512]{1,0:T(8,128)(2,1)S(1)} %get-tuple-element.12.k, bf16[512,512]{1,0:T(8,128)(2,1)S(1)} %get-tuple-element.13.v, ...), custom_call_target="tpu_custom_call" | custom-call | tf_op jit(solution)/shard_map/finish/pallas_call | solution.py:468

commit v7 on v6

--- a/solution.py
+++ b/solution.py
@@ -153,28 +153,19 @@
             device_id=(other, y), device_id_type=MESH,
         )
 
-    columns = sorted(range(lines), key=lambda d: -min(d, lines - d))
-    columns = [(x + d) % lines for d in columns]
+    def apart(d, size):
+        return min(d, size - d)
+
+    offsets = [(a, b) for a in range(planes) for b in range(lines) if a or b]
+    offsets.sort(key=lambda o: -apart(o[0], planes) - apart(o[1], lines))
 
     def to_chips(src, dst, send, recv, index):
-        def one(j):
+        for a, b in offsets:
+            j = (z + a) % planes * lines + (x + b) % lines
             pltpu.make_async_remote_copy(
                 src_ref=src.at[index(j)], dst_ref=dst.at[chip], send_sem=send, recv_sem=recv,
                 device_id=(j * 2 + core, y), device_id_type=MESH,
             ).start()
-
-        def row(n, c):
-            there = (z + far_first(n, planes)) % planes * lines
-            for line in columns[:-1]:
-                one(there + line)
-
-            @pl.when(n < planes - 1)
-            def _():
-                one(there + columns[-1])
-
-            return c
-
-        lax.fori_loop(0, planes, row, 0)
 
     def arrived(ref, count, sem):
         part = ref.at[pl.ds(0, count)]
@@ -298,23 +289,16 @@
         to_left[half - 1 - c].wait_recv()
         add(2, half - 1 - c)
 
-    heads = (1 - core, core)
-    for h in range(2):
-        own[1, h] = jnp.zeros((size, size), F32)
     for c in range(half):
         for at in (c, CHUNKS - 1 - c):
             onward[at].wait_recv()
             span = slice(at * chunk, (at + 1) * chunk)
             g_v[span, :] = (acc[span, :] + nn(og_v[3, span], w_t[2])).astype(BF16)
-        for i in range(2):
-            at = pl.ds(pl.multiple_of(heads[i] * size, 128), size)
-            total = own[1, heads[i]]
-            for r in (c, CHUNKS - 1 - c):
-                span = slice(r * chunk, (r + 1) * chunk)
-                total = total + nn(dq[heads[i], :, span], g_v[span, at])
-            own[1, heads[i]] = total
-            if c == half - 1 and i == 0:
-                first_send(1)
+    for h in (1 - core, core):
+        at = pl.ds(pl.multiple_of(h * size, 128), size)
+        own[1, h] = nn(dq[h], g_v[:, at])
+        if h is not core:
+            first_send(1)
 
     outs = [pltpu.make_async_copy(oc_v, outflow, out_sem.at[3, 0])]
     for i, (src, dst) in enumerate(((k_v, k_out), (v_v, v_out))):
@@ -358,9 +342,8 @@
         outs.append(pltpu.make_async_copy(src.at[:, theirs], dst.at[:, theirs], out_sem.at[1 + i, 0]))
         outs[-1].start()
     entering = fourth_send(1)
-    kg_v[:, mine] += outc[core] * nt(v_v[:, mine], entering)
-    vg_v[:, mine] += outc[core] * nn(k_v[:, mine], entering)
     for i, (src, dst) in enumerate(((kg_v, kg), (vg_v, vg))):
+        src[:, mine] += outc[core] * (nn(k_v[:, mine], entering) if i else nt(v_v[:, mine], entering))
         outs.append(pltpu.make_async_copy(src.at[:, mine], dst.at[:, mine], out_sem.at[1 + i, 1]))
         outs[-1].start()
     arrived(en_send.at[1], chips - 1, c_send.at[1, 2])

time: 51.2 us -> 51.4 us (level)
  no operation moved by 1% of the time
where the time goes in v7:
time: 51.4 us; the launch traced here: 51.3 us
  Pallas kernels  50.6 us (98%)
  between operations  0.64 us (1%)
    pallas_call x1, Pallas kernels, on_device(): pl.pallas_call(functools.partial(kernel, planes, lines), out_shape=tuple(...  48.9 us
    pallas_call x1, Pallas kernels, on_device(): pl.pallas_call(finish, out_shape=(result, result, result), in_specs=[pl.B...  1.77 us

profile of v7, /device:TPU:1, one launch (start us, length us, event | category | flops | bytes accessed | tf_op | source)
XLA Modules:
  0.0 51.3 jit_solution(7176527577000730640)
XLA Ops:
  0.6 48.9 %retention_backward.1 = (f32[512,512]{1,0:T(8,128)S(1)}, f32[512,512]{1,0:T(8,128)S(1)}, f32[512,512]{1,0:T(8,128)S(1)}, bf16[256,256]{1,0:T(8,128)(2,1)S(1)}, f...) custom-call(s32[3]{0:T(128)} %doc_in.1, f32[2,512]{1,0:T(2,128)} %ld_in.1, ...), custom_call_target="tpu_custom_call" | custom-call | tf_op jit(solution)/shard_map/retention_backward/pallas_call | solution.py:437
  49.5 1.8 %finish.1 = (f32[512,512]{1,0:T(8,128)}, f32[512,512]{1,0:T(8,128)}, f32[512,512]{1,0:T(8,128)}) custom-call(bf16[256,256]{1,0:T(8,128)(2,1)S(1)} %get-tuple-element.10.adjoint, f32[512,128]{1,0:T(8,128)S(1)} %get-tuple-element.11.outflow, bf16[512,512]{1,0:T(8,128)(2,1)S(1)} %get-tuple-element.12.k, bf16[512,512]{1,0:T(8,128)(2,1)S(1)} %get-tuple-element.13.v, ...), custom_call_target="tpu_custom_call" | custom-call | tf_op jit(solution)/shard_map/finish/pallas_call | solution.py:451

commit v8 on v7

--- a/solution.py
+++ b/solution.py
@@ -8,7 +8,7 @@
 from jax.sharding import PartitionSpec as P
 
 PLANE = 4
-CHUNKS = 4
+CHUNKS = 8
 MESH = pl.DeviceIdType.MESH
 F32 = jnp.float32
 BF16 = jnp.bfloat16
@@ -91,7 +91,7 @@
     def hop(src_slot, dst_slot, c, to, lane):
         at = pl.ds(c * chunk, chunk)
         return pltpu.make_async_remote_copy(
-            src_ref=og_v.at[src_slot, at], dst_ref=og_v.at[dst_slot, at],
+            src_ref=og_v.at[src_slot, at] if src_slot else og.at[at], dst_ref=og_v.at[dst_slot, at],
             send_sem=y_send.at[lane, c], recv_sem=y_rec.at[dst_slot - 1, c],
             device_id=(ctx, to), device_id_type=MESH,
         )
@@ -99,7 +99,6 @@
     to_right = [hop(0, 1, c, right, 0) for c in range(CHUNKS)]
     to_left = [hop(0, 2, c, left, 1) for c in range(CHUNKS)]
     onward = [hop(1, 3, c, right, 2) if c < CHUNKS // 2 else hop(2, 3, c, left, 2) for c in range(CHUNKS)]
-    loads[0].wait()
     for c in range(CHUNKS):
         to_right[c].start()
         to_left[CHUNKS - 1 - c].start()
@@ -259,6 +258,7 @@
         sm[h] = (nt(q_v[:, cols(h)], k_v[:, cols(h)]) * wt[h]).astype(BF16)
     hear(1)
     tell(2)
+    loads[0].wait()
     loads[4].wait()
     acc[...] = nt(og_v[0], w_v[0])
     for i in range(1, 4):

time: 51.4 us -> 51.9 us (level)
  no operation moved by 1% of the time
where the time goes in v8:
time: 51.9 us; the launch traced here: 51.8 us
  Pallas kernels  51.1 us (98%)
  between operations  0.64 us (1%)
    pallas_call x1, Pallas kernels, on_device(): pl.pallas_call(functools.partial(kernel, planes, lines), out_shape=tuple(...  49.4 us
    pallas_call x1, Pallas kernels, on_device(): pl.pallas_call(finish, out_shape=(result, result, result), in_specs=[pl.B...  1.77 us

profile of v8, /device:TPU:1, one launch (start us, length us, event | category | flops | bytes accessed | tf_op | source)
XLA Modules:
  0.0 51.8 jit_solution(4565446527693821047)
XLA Ops:
  0.6 49.4 %retention_backward.1 = (f32[512,512]{1,0:T(8,128)S(1)}, f32[512,512]{1,0:T(8,128)S(1)}, f32[512,512]{1,0:T(8,128)S(1)}, bf16[256,256]{1,0:T(8,128)(2,1)S(1)}, f...) custom-call(s32[3]{0:T(128)} %doc_in.1, f32[2,512]{1,0:T(2,128)} %ld_in.1, ...), custom_call_target="tpu_custom_call" | custom-call | tf_op jit(solution)/shard_map/retention_backward/pallas_call | solution.py:437
  50.0 1.8 %finish.1 = (f32[512,512]{1,0:T(8,128)}, f32[512,512]{1,0:T(8,128)}, f32[512,512]{1,0:T(8,128)}) custom-call(bf16[256,256]{1,0:T(8,128)(2,1)S(1)} %get-tuple-element.10.adjoint, f32[512,128]{1,0:T(8,128)S(1)} %get-tuple-element.11.outflow, bf16[512,512]{1,0:T(8,128)(2,1)S(1)} %get-tuple-element.12.k, bf16[512,512]{1,0:T(8,128)(2,1)S(1)} %get-tuple-element.13.v, ...), custom_call_target="tpu_custom_call" | custom-call | tf_op jit(solution)/shard_map/finish/pallas_call | solution.py:451
